TPU v7x, 1024 devices: a whole 4x8x16 slice. The times are simulated.
1024 devices in a mesh: section: 16 (over y_hi, x), dp: 64 (over y_lo, z, core).
Axes of the slice: x: 4, y: 8 (y_hi: 4, y_lo: 2; y = y_hi * 2 + y_lo), z: 16, core: 2. Of those that a mesh axis runs over, the one named last changes fastest.
Arguments:
- counts: int32 [16], replicated, may hold values from 1 to 3, 32 in all
- activations: bfloat16 [16, 3, 8192, 1792], P('section', None, 'dp'), may hold values from -16 to 16
- cotangents: bfloat16 [16, 3, 8192, 64], P('section', None, 'dp'), may hold values from -1 to 1
Outputs:
- clipped: float32 [32, 1792, 64], P('section', 'dp')
Inputs may be any that keep to these rules, and one draw needn't show every extreme that they name: The counts sum to 32; the largest is 3.
All inputs are finite; a program needn't handle non-finite values.
Results may differ from a plain program's by a relative error of at most 0.003.
Values sent between devices are 32-bit elements; how exact they have to be, the bound alone decides.
No kernel may reach another device: no remote copies, remote signals or barrier semaphores. Data moves between devices by JAX's collectives and lax.ppermute only.
A program may use at most 32 MiB of HBM per device.

v0:
```python
import jax
import jax.numpy as jnp
from jax import lax
from jax.sharding import PartitionSpec as P

DEPTHS_PER_OWNER = 2


def on_device(counts, activations, cotangents):
    inputs_here = activations[0]
    local_cotangent = cotangents[0]
    number_of_slots = inputs_here.shape[0]
    hidden_width = inputs_here.shape[2]
    adapter_rank = local_cotangent.shape[2]
    replica_count = lax.axis_size("dp")
    number_of_sections = lax.axis_size("section")
    total_depths = number_of_sections * DEPTHS_PER_OWNER
    rows_per_section = hidden_width // replica_count
    section_here = lax.axis_index("section")
    offsets = jnp.cumsum(counts) - counts
    slot_ids = jnp.arange(number_of_slots, dtype=jnp.int32)
    active_mask = (slot_ids < counts[section_here]).astype(jnp.float32)
    outer_product = jnp.einsum(
        "ktd,ktr->dkr", inputs_here, local_cotangent, preferred_element_type=jnp.float32
    )
    summed_gradient = lax.psum_scatter(
        outer_product.reshape(
            lax.axis_size("dp") * rows_per_section, number_of_slots * adapter_rank
        ),
        "dp",
        scatter_dimension=0,
        tiled=True,
    )
    summed_gradient = (
        summed_gradient.reshape(rows_per_section, number_of_slots, adapter_rank)
        * active_mask[None, :, None]
    )
    owned_ids = section_here * DEPTHS_PER_OWNER + jnp.arange(DEPTHS_PER_OWNER, dtype=jnp.int32)
    depth_ids = (offsets[:, None] + slot_ids[None, :] + total_depths // 2) % total_depths
    valid_slot = slot_ids[None, :] < counts[:, None]
    selector = (
        (depth_ids[:, :, None] == owned_ids[None, None, :]) & valid_slot[:, :, None]
    ).astype(jnp.float32)
    owned_tiles = jnp.einsum(
        "nke,nrkc->erc",
        selector,
        lax.all_gather(summed_gradient[None], "section", axis=0, tiled=True),
        precision=lax.Precision.HIGHEST,
    )
    square_sum = lax.psum(jnp.sum(owned_tiles * owned_tiles), ("section", "dp"))
    count_of_entries = number_of_sections * DEPTHS_PER_OWNER * hidden_width * adapter_rank
    factor = jnp.minimum(1.0, 0.5 / jnp.sqrt(square_sum / count_of_entries + 1e-06))
    return owned_tiles * factor


def solution(mesh):
    return jax.shard_map(
        on_device,
        mesh=mesh,
        in_specs=(P(), P("section", None, "dp", None), P("section", None, "dp", None)),
        out_specs=P("section", "dp", None),
        check_vma=False,
    )
```

profile of v0, /device:TPU:1, one launch (start us, length us, event | category | flops | bytes accessed | tf_op | source)
XLA Modules:
  0.0 630.0 jit_solution(1688263830159180312)
XLA Ops:
  6.5 0.0 copy-start
  6.5 0.0 all-reduce.3.cloned.1.call-start
  6.5 1.3 copy-done
  7.9 2.2 fusion
  10.1 0.0 copy-start.1
  10.1 0.0 all-reduce.3.cloned.1.call-update
  10.2 0.6 copy-done.1
  10.8 0.6 dynamic_slice.3
  11.4 0.1 copy.8
  11.5 0.1 reduce
  11.7 1.3 dynamic-slice
  13.6 0.7 compare_convert_fusion
  14.3 438.1 %all-reduce.3.cloned.1.call-done = f32[1792,192]{0,1:T(8,128)} async-done(((f32[1792,192]{0,1:T(8,128)}), f32[1792,192]{0,1:T(8,128)}) %all-reduce.3.cloned.1.call-update) | async-done | bytes 1376272
  452.4 1.0 constant_dynamic-slice_fusion
  453.4 0.1 copy.9
  453.5 0.1 broadcast_multiply_fusion
  453.6 40.7 %all_gather.3 = f32[16,28,3,64]{3,1,2,0:T(8,128)S(1)} all-gather(f32[1,28,3,64]{3,1,2,0:T(8,128)S(1)} %broadcast_multiply_fusion), channel_id=1, replica_groups=mesh['section'=16,'dp'=64] {'section'}, dimensions={0}, use_global_device_ids=true | all-gather | bytes 365568 | tf_op jit(solution)/shard_map/all_gather | solution.py:47
  494.3 1.4 multiply_reduce_fusion
  495.7 126.2 %psum.7 = f32[]{:T(128)} all-reduce(f32[]{:T(128)} %get-tuple-element.5), channel_id=1, replica_groups=mesh['section'=16,'dp'=64] {'section','dp'}, use_global_device_ids=true, to_apply=%region_3.4 | all-reduce | flops 1 | bytes 8 | tf_op jit(solution)/shard_map/psum | solution.py:50
  622.6 0.6 broadcast_multiply_fusion.1
  (5 shorter events, 0.1 us)
Async XLA Ops:
  6.5 1.3 copy-start
  6.5 445.9 %all-reduce.3.cloned.1.call-start = ((), (), s32[]{:S(2)}) async-start(), calls=%async_computation | async-start | bytes 2752512
  10.1 0.7 copy-start.1
Sparse Core Ops, SparseCore 0:
  10.9 441.5 all-reduce.2
where the time goes:
time: 630 us
  waiting for transfers between devices  438 us (70%)
  blocking collectives  167 us (27%)
  between operations  14.8 us (2%)
    unnamed x2, waiting for transfers between devices  438 us
    psum x1, blocking collectives, on_device(): square_sum = lax.psum(jnp.sum(owned_tiles * owned_tiles), ('section', 'dp'))  126 us
    all_gather x1, blocking collectives, on_device(): lax.all_gather(summed_gradient[None], 'section', axis=0, tiled=True)  40.7 us
  transfers between devices with their start and end apart: 1, of which 1 were waited for; matrix products, arithmetic and copies ran while one was open for 0% of the time, Pallas kernels for 0%

commit v1 on v0

v1 whole, which is shorter than its diff:
```python
import functools

import jax
import jax.numpy as jnp
from jax import lax
from jax.experimental import pallas as pl
from jax.experimental.pallas import tpu as pltpu
from jax.sharding import Mesh, PartitionSpec as P

DEPTHS_PER_OWNER = 2
Y_PAIR = 2
CORES = 2
LANES = 128
PAD_ROWS = 16
VMEM = pl.BlockSpec(memory_space=pltpu.VMEM)
SMEM = pl.BlockSpec(memory_space=pltpu.SMEM)


def call(body, shapes, in_specs, scratch=()):
    return pl.pallas_call(
        body,
        out_shape=tuple(jax.ShapeDtypeStruct(s, jnp.float32) for s in shapes),
        in_specs=in_specs,
        out_specs=tuple(VMEM for _ in shapes),
        scratch_shapes=list(scratch),
        compiler_params=pltpu.CompilerParams(vmem_limit_bytes=24 * 1024 * 1024),
    )


def partial_kernel(slots, tokens, rank, chunk, place, a_ref, c_ref, keep_ref, send_ref, p_ref):
    width = 2 * slots * rank
    lane = lax.broadcasted_iota(jnp.int32, (rank, width), 1)
    row = lax.broadcasted_iota(jnp.int32, (rank, width), 0)
    spread = (lane % rank == row).astype(jnp.bfloat16)
    tiled = jnp.dot(c_ref[...], spread, preferred_element_type=jnp.float32)
    lane = lax.broadcasted_iota(jnp.int32, (slots * tokens, width), 1)
    row = lax.broadcasted_iota(jnp.int32, (slots * tokens, width), 0)
    own = (lane // rank) % slots == row // tokens
    blocks = jnp.where(own, tiled, 0.0).astype(jnp.bfloat16)
    p_ref[...] = lax.dot_general(
        a_ref[...], blocks, (((0,), (0,)), ((), ())), preferred_element_type=jnp.float32
    )
    half = chunk // 2
    left = lax.broadcasted_iota(jnp.int32, (half, width), 1) < slots * rank
    groups = keep_ref.shape[0] // half

    def pack(core, out_ref):
        for i in range(groups):
            start = (CORES * i + core) * chunk
            out_ref[pl.ds(half * i, half), :] = jnp.where(
                left, p_ref[pl.ds(start, half), :], p_ref[pl.ds(start + half, half), :]
            )

    core = place[2]

    @pl.when(core == 0)
    def _():
        pack(1, send_ref)
        pack(0, keep_ref)

    @pl.when(core == 1)
    def _():
        pack(0, send_ref)
        pack(1, keep_ref)


def pair_send_kernel(place, keep_ref, got_ref, send_ref):
    rows = send_ref.shape[0]
    there = pl.ds(pl.multiple_of((1 - place[1]) * rows, 8), rows)
    send_ref[...] = keep_ref[there, :] + got_ref[there, :]


def ring_send_kernel(place, keep_ref, got_ref, pair_ref, ring_ref):
    rows = pair_ref.shape[0]
    here = pl.ds(pl.multiple_of(place[1] * rows, 8), rows)
    total = keep_ref[here, :] + got_ref[here, :] + pair_ref[...]
    count, _, width = ring_ref.shape
    half = rows // count
    blank = jnp.zeros((PAD_ROWS - half, width), jnp.float32)
    for i in range(count):
        ring_ref[i, pl.ds(0, half), :] = total[i * half : (i + 1) * half, :]
        ring_ref[i, pl.ds(half, PAD_ROWS - half), :] = blank


def route_kernel(slots, rank, place, counts, ring_ref, out_ref):
    owners, rows, _ = out_ref.shape
    width = ring_ref.shape[2]
    section = place[0]
    offset = jnp.int32(0)
    for s in range(owners):
        offset = offset + jnp.where(s < section, counts[s], 0)
    live = counts[section]
    total = jnp.sum(ring_ref[...], axis=0)
    lane = lax.broadcasted_iota(jnp.int32, (rows, width), 1)
    total = jnp.where((lane // rank) % slots < live, total, 0.0)
    square = jnp.sum(total * total)
    last = lax.broadcasted_iota(jnp.int32, (rows, 2 * LANES), 0) == rows - 1
    out_ref[...] = jnp.broadcast_to(jnp.where(last, square, 0.0)[None], out_ref.shape)
    side = lax.broadcasted_iota(jnp.int32, (rows, LANES), 1) // rank
    depths = owners * DEPTHS_PER_OWNER
    for k in range(slots):
        depth = lax.rem(offset + k + depths // 2, depths)
        owner = depth // DEPTHS_PER_OWNER
        spot = depth - owner * DEPTHS_PER_OWNER

        @pl.when(k < live)
        def _():
            for h in range(2):
                block = h * slots + k
                tile = total[:, (block // 2) * LANES : (block // 2 + 1) * LANES]
                turned = pltpu.roll(tile, rank, 1)
                value = jnp.where(side == block % 2, tile, 0.0)
                moved = jnp.where(side != block % 2, turned, 0.0)
                at = (owner, slice(None), pl.ds(h * LANES, LANES))
                out_ref[at] = out_ref[at] + jnp.where(spot == block % 2, value, moved)


def own_kernel(got_ref, owned_ref, square_ref):
    total = jnp.sum(got_ref[...], axis=0)
    owned_ref[...] = total
    square_ref[...] = jnp.broadcast_to(total[total.shape[0] - 1 :, :LANES], square_ref.shape)


def clip_kernel(entries, rank, owned_ref, squares_ref, out_ref):
    total = jnp.sum(squares_ref[...], axis=0)
    factor = jnp.minimum(1.0, 0.5 / jnp.sqrt(total / entries + 1e-06))
    half = out_ref.shape[1] // 2
    factor = jnp.broadcast_to(factor[:1, :], (half, LANES))
    for h in range(2):
        tile = owned_ref[pl.ds(0, half), pl.ds(h * LANES, LANES)] * factor
        turned = pltpu.roll(owned_ref[:, pl.ds(h * LANES, LANES)], rank, 1)[:half] * factor
        out_ref[0, pl.ds(half * h, half), :] = tile[:, :rank]
        out_ref[1, pl.ds(half * h, half), :] = turned[:, :rank]


def on_device(counts, activations, cotangents):
    _, slots, tokens, hidden = activations.shape
    rank = cotangents.shape[3]
    sections, ring = lax.axis_size("section"), lax.axis_size("ring")
    chunk = hidden // (Y_PAIR * ring * CORES)
    width = 2 * slots * rank
    half = chunk // 2
    place = jnp.stack(
        [lax.axis_index("section"), lax.axis_index("pair"), lax.axis_index("core")]
    ).astype(jnp.int32)
    rows = Y_PAIR * ring * half
    swap = [(0, 1), (1, 0)]
    with jax.named_scope("partials"):
        keep, send = call(
            functools.partial(partial_kernel, slots, tokens, rank, chunk),
            [(rows, width)] * 2,
            [SMEM, VMEM, VMEM],
            [pltpu.VMEM((hidden, width), jnp.float32)],
        )(
            place,
            activations.reshape(slots * tokens, hidden),
            cotangents.reshape(slots * tokens, rank),
        )
    with jax.named_scope("core_sum"):
        got = lax.ppermute(send, "core", swap)
    with jax.named_scope("pair_sum"):
        (send,) = call(pair_send_kernel, [(rows // 2, width)], [SMEM, VMEM, VMEM])(place, keep, got)
        pair = lax.ppermute(send, "pair", swap)
    with jax.named_scope("ring_sum"):
        (blocks,) = call(ring_send_kernel, [(ring, PAD_ROWS, width)], [SMEM, VMEM, VMEM, VMEM])(
            place, keep, got, pair
        )
        blocks = lax.all_to_all(blocks, "ring", 0, 0, tiled=True)
    with jax.named_scope("route"):
        (routed,) = call(
            functools.partial(route_kernel, slots, rank),
            [(sections, PAD_ROWS, 2 * LANES)],
            [SMEM, SMEM, VMEM],
        )(place, counts, blocks)
        routed = lax.all_to_all(routed, "section", 0, 0, tiled=True)
        owned, square = call(own_kernel, [(PAD_ROWS, 2 * LANES), (8, LANES)], [VMEM])(routed)
    with jax.named_scope("norm"):
        square = lax.psum(square, "core")
        squares = jnp.broadcast_to(square[None], (Y_PAIR * ring, 8, LANES))
        squares = lax.all_to_all(squares, ("pair", "ring"), 0, 0, tiled=True)
    with jax.named_scope("clip"):
        entries = sections * DEPTHS_PER_OWNER * hidden * rank
        (out,) = call(
            functools.partial(clip_kernel, entries, rank),
            [(DEPTHS_PER_OWNER, chunk, rank)],
            [VMEM, VMEM],
        )(owned, squares)
    return out


def solution(mesh):
    sections, replicas = mesh.devices.shape
    split = Mesh(
        mesh.devices.reshape(sections, Y_PAIR, replicas // (Y_PAIR * CORES), CORES),
        ("section", "pair", "ring", "core"),
    )
    dp = ("pair", "ring", "core")
    return jax.shard_map(
        on_device,
        mesh=split,
        in_specs=(P(), P("section", None, dp, None), P("section", None, dp, None)),
        out_specs=P("section", dp, None),
        check_vma=False,
    )
```

time: 630 us -> 112 us (0.18)
  waiting for transfers between devices: 438 us -> 11 us
  blocking collectives: 167 us -> 75.4 us
  starting transfers between devices: 0.01 us -> 18 us
  between operations: 14.8 us -> 0.07 us
    unnamed x2 -> x0, waiting for transfers between devices: 438 us -> none
    psum x1, blocking collectives: 126 us -> 10.2 us  [on_device(): square = lax.psum(square, 'core')]
    all_to_all x0 -> x3, blocking collectives: none -> 65.2 us  [the longest x1 23.2 us: on_device(): blocks = lax.all_to_all(blocks, 'ring', 0, 0, tiled=True)]
    all_gather x1 -> x0, blocking collectives: 40.7 us -> none  [on_device(): lax.all_gather(summed_gradient[None], 'section', axis=0, tiled=True)]
    ppermute x0 -> x2, starting transfers between devices: none -> 18 us  [the longest x1 16.1 us: on_device(): got = lax.ppermute(send, 'core', swap)]
    ppermute x0 -> x2, waiting for transfers between devices: none -> 11 us  [the longest x1 9.24 us: on_device(): pair = lax.ppermute(send, 'pair', swap)]
  transfers between devices with their start and end apart: 1 -> 2, of which waited for: 1 -> 2; matrix products, arithmetic and copies ran while one was open for 0% -> 0% of each run, Pallas kernels for 0% -> 0%
where the time goes in v1:
time: 112 us; the launch traced here: 111 us
  blocking collectives  75.4 us (67%)
  starting transfers between devices  18 us (16%)
  waiting for transfers between devices  11 us (10%)
  Pallas kernels  3.97 us (4%)
  local copies, waits for them, and re-layouts  2.91 us (3%)
    all_to_all x1, blocking collectives, on_device(): blocks = lax.all_to_all(blocks, 'ring', 0, 0, tiled=True)  23.2 us
    all_to_all x1, blocking collectives, on_device(): squares = lax.all_to_all(squares, ('pair', 'ring'), 0, 0, tiled=True)  22.7 us
    all_to_all x1, blocking collectives, on_device(): routed = lax.all_to_all(routed, 'section', 0, 0, tiled=True)  19.2 us
    ppermute x1, starting transfers between devices, on_device(): got = lax.ppermute(send, 'core', swap)  16.1 us
    psum x1, blocking collectives, on_device(): square = lax.psum(square, 'core')  10.2 us
    ppermute x1, waiting for transfers between devices, on_device(): pair = lax.ppermute(send, 'pair', swap)  9.24 us
    unnamed x5, local copies, waits for them, and re-layouts  2.26 us
  transfers between devices with their start and end apart: 2, of which 2 were waited for; matrix products, arithmetic and copies ran while one was open for 0% of the time, Pallas kernels for 0%

profile of v1, /device:TPU:1, one launch (start us, length us, event | category | flops | bytes accessed | tf_op | source)
XLA Modules:
  0.0 111.4 jit_solution(4322762347043065847)
XLA Ops:
  0.0 0.9 copy.4
  0.9 0.1 pad_add_fusion.place
  1.0 0.0 copy-start
  1.0 1.3 %copy-done = bf16[1,3,128,1792]{3,2,1,0:T(8,128)(2,1)S(1)} copy-done((bf16[1,3,128,1792]{3,2,1,0:T(8,128)(2,1)S(1)}, bf16[1,3,128,1792]{3,2,1,0:T(8,128)(2,1)}, u32[]{:S(2)}) %copy-start) | copy-done | bytes 1376280
  2.3 2.0 %partials.1 = (f32[448,384]{1,0:T(8,128)S(1)}, f32[448,384]{1,0:T(8,128)S(1)}) custom-call(s32[3]{0:T(128)S(1)} %pad_add_fusion.place, bf16[384,1792]{1,0:T(8,128)(2,1)S(1)} %bitcast.5, bf16[384,64]{1,0:T(8,128)(2,1)S(1)} %bitcast.6), custom_call_target="tpu_custom_call" | custom-call | tf_op jit(solution)/shard_map/partials/pallas_call | solution.py:149
  4.3 16.1 %collective-permute-start = (f32[448,384]{1,0:T(8,128)S(1)}, f32[448,384]{1,0:T(8,128)S(1)}, u32[]{:S(2)}, u32[]{:S(2)}) collective-permute-start(f32[448,384]{1,0:T(8,128)S(1)} %get-tuple-element.10), channel_id=1, source_target_pairs={{0,1},{1,0},{2,3},{3,2},{4,5},{5,4},{6,7},{7,6},{8,9},{9,8},{10,11... | collective-permute-start | bytes 2064392 | tf_op jit(solution)/shard_map/core_sum/ppermute | solution.py:160
  20.4 1.7 %collective-permute-done.got_ref = f32[448,384]{1,0:T(8,128)S(1)} collective-permute-done((f32[448,384]{1,0:T(8,128)S(1)}, f32[448,384]{1,0:T(8,128)S(1)}, u32[]{:S(2)}, u32[]{:S(2)}) %collective-permute-start) | collective-permute-done | bytes 688160 | tf_op jit(solution)/shard_map/core_sum/ppermute | solution.py:160
  22.1 0.6 pair_sum.1
  22.7 0.0 copy-start.1
  22.7 1.9 %collective-permute-start.1 = (f32[224,384]{1,0:T(8,128)S(1)}, f32[224,384]{1,0:T(8,128)S(1)}, u32[]{:S(2)}, u32[]{:S(2)}) collective-permute-start(f32[224,384]{1,0:T(8,128)S(1)} %pair_sum.1), channel_id=1, source_target_pairs={{0,32},{32,0},{1,33},{33,1},{2,34},{34,2},{3,35},{35,3},{4,36},{36... | collective-permute-start | bytes 1032200 | tf_op jit(solution)/shard_map/pair_sum/ppermute | solution.py:163
  24.7 9.2 %collective-permute-done.1.pair_ref = f32[224,384]{1,0:T(8,128)S(1)} collective-permute-done((f32[224,384]{1,0:T(8,128)S(1)}, f32[224,384]{1,0:T(8,128)S(1)}, u32[]{:S(2)}, u32[]{:S(2)}) %collective-permute-start.1) | collective-permute-done | bytes 344096 | tf_op jit(solution)/shard_map/pair_sum/ppermute | solution.py:163
  33.9 0.6 ring_sum.1
  34.5 23.2 %all_to_all.15.ring_ref = f32[16,16,384]{2,1,0:T(8,128)S(1)} all-to-all(f32[16,16,384]{2,1,0:T(8,128)S(1)} %ring_sum.1), channel_id=1, replica_groups=mesh['section'=16,'pair'=2,'ring'=16,'core'=2] {'ring'}, dimensions={0} | all-to-all | bytes 786432 | tf_op jit(solution)/shard_map/ring_sum/all_to_all | solution.py:168
  57.8 0.0 copy-done.1
  57.8 0.7 route.2
  58.5 19.2 %all_to_all.16.got_ref = f32[16,16,256]{2,1,0:T(8,128)S(1)} all-to-all(f32[16,16,256]{2,1,0:T(8,128)S(1)} %route.2), channel_id=1, replica_groups=mesh['section'=16,'pair'=2,'ring'=16,'core'=2] {'section'}, dimensions={0} | all-to-all | bytes 524288 | tf_op jit(solution)/shard_map/route/all_to_all | solution.py:175
  77.8 10.2 %psum.7 = f32[8,128]{1,0:T(8,128)S(1)} all-reduce(f32[8,128]{1,0:T(8,128)S(1)} %get-tuple-element.12), channel_id=1, replica_groups=mesh['section'=16,'pair'=2,'ring'=16,'core'=2] {'core'}, use_global_device_ids=true, to_apply=%region_0.0 | all-reduce | flops 1024 | bytes 8192 | tf_op jit(solution)/shard_map/norm/psum | solution.py:178
  88.0 22.7 %all_to_all.17.squares_ref = f32[32,8,128]{2,1,0:T(8,128)S(1)} all-to-all(f32[32,8,128]{2,1,0:T(8,128)S(1)} %broadcast_in_dim.2), channel_id=1, replica_groups=mesh['section'=16,'pair'=2,'ring'=16,'core'=2] {'pair','ring'}, dimensions={0} | all-to-all | bytes 262144 | tf_op jit(solution)/shard_map/norm/all_to_all | solution.py:180
  110.7 0.1 clip.1
  110.7 0.6 copy.5
  (2 shorter events, 0.0 us)
Async XLA Ops:
  1.0 1.3 %copy-start = (bf16[1,3,128,1792]{3,2,1,0:T(8,128)(2,1)S(1)}, bf16[1,3,128,1792]{3,2,1,0:T(8,128)(2,1)}, u32[]{:S(2)}) copy-start(bf16[1,3,128,1792]{3,2,1,0:T(8,128)(2,1)} %param.4) | copy-start | bytes 4128772
  4.3 17.8 %collective-permute-start = (f32[448,384]{1,0:T(8,128)S(1)}, f32[448,384]{1,0:T(8,128)S(1)}, u32[]{:S(2)}, u32[]{:S(2)}) collective-permute-start(f32[448,384]{1,0:T(8,128)S(1)} %get-tuple-element.10), channel_id=1, source_target_pairs={{0,1},{1,0},{2,3},{3,2},{4,5},{5,4},{6,7},{7,6},{8,9},{9,8},{10,11... | collective-permute-start | bytes 2064392 | tf_op jit(solution)/shard_map/core_sum/ppermute | solution.py:160
  22.7 35.0 %copy-start.1 = (s32[16]{0:T(128)S(1)}, s32[16]{0:T(128)}, u32[]{:S(2)}) copy-start(s32[16]{0:T(128)} %counts.1) | copy-start | bytes 196
  22.7 11.2 %collective-permute-start.1 = (f32[224,384]{1,0:T(8,128)S(1)}, f32[224,384]{1,0:T(8,128)S(1)}, u32[]{:S(2)}, u32[]{:S(2)}) collective-permute-start(f32[224,384]{1,0:T(8,128)S(1)} %pair_sum.1), channel_id=1, source_target_pairs={{0,32},{32,0},{1,33},{33,1},{2,34},{34,2},{3,35},{35,3},{4,36},{36... | collective-permute-start | bytes 1032200 | tf_op jit(solution)/shard_map/pair_sum/ppermute | solution.py:163

commit v2 on v1

v2 whole, which is shorter than its diff:
```python
import functools

import jax
import jax.numpy as jnp
from jax import lax
from jax.experimental import pallas as pl
from jax.experimental.pallas import tpu as pltpu
from jax.sharding import Mesh, PartitionSpec as P

DEPTHS_PER_OWNER = 2
Y_PAIR = 2
NEAR = 2
CORES = 2
LANES = 128
PAD_ROWS = 16
VMEM = pl.BlockSpec(memory_space=pltpu.VMEM)
SMEM = pl.BlockSpec(memory_space=pltpu.SMEM)


def call(body, shapes, in_specs, scratch=()):
    return pl.pallas_call(
        body,
        out_shape=tuple(jax.ShapeDtypeStruct(s, jnp.float32) for s in shapes),
        in_specs=in_specs,
        out_specs=tuple(VMEM for _ in shapes),
        scratch_shapes=list(scratch),
        compiler_params=pltpu.CompilerParams(vmem_limit_bytes=24 * 1024 * 1024),
    )


def partial_kernel(chunk, far, place, a_ref, c_ref, keep_ref, send_ref, p_ref):
    slots, rank, tokens = c_ref.shape
    width = 2 * slots * rank
    lane = lax.broadcasted_iota(jnp.int32, (rank, width), 1)
    row = lax.broadcasted_iota(jnp.int32, (rank, width), 0)
    spread = (lane % rank == row).astype(jnp.bfloat16)
    slot = (lax.broadcasted_iota(jnp.int32, (tokens, width), 1) // rank) % slots
    over_rows = (((0,), (0,)), ((), ()))
    blocks = []
    for k in range(slots):
        tiled = lax.dot_general(c_ref[k], spread, over_rows, preferred_element_type=jnp.float32)
        blocks.append(jnp.where(slot == k, tiled, 0.0).astype(jnp.bfloat16))
    p_ref[...] = lax.dot_general(
        a_ref[...],
        jnp.concatenate(blocks, axis=0),
        over_rows,
        preferred_element_type=jnp.float32,
    )
    half = chunk // 2
    left = lax.broadcasted_iota(jnp.int32, (half, width), 1) < slots * rank

    def pack(core, out_ref):
        at = 0
        for pair in range(Y_PAIR):
            for near in range(NEAR):
                for step in range(far):
                    start = (((pair * far + step) * NEAR + near) * CORES + core) * chunk
                    out_ref[pl.ds(at, half), :] = jnp.where(
                        left, p_ref[pl.ds(start, half), :], p_ref[pl.ds(start + half, half), :]
                    )
                    at += half

    core = place[1]

    @pl.when(core == 0)
    def _():
        pack(1, send_ref)
        pack(0, keep_ref)

    @pl.when(core == 1)
    def _():
        pack(0, send_ref)
        pack(1, keep_ref)


def core_sum_kernel(keep_ref, got_ref, out_ref):
    groups, rows, _ = out_ref.shape
    for i in range(groups):
        at = pl.ds(i * rows, rows)
        out_ref[i] = keep_ref[at, :] + got_ref[at, :]


def near_sum_kernel(got_ref, out_ref):
    total = jnp.sum(got_ref[...], axis=0)
    far = out_ref.shape[0]
    half, tiles = total.shape[0] // far, total.shape[1] // LANES
    for i in range(far):
        for r in range(half):
            for t in range(tiles):
                piece = total[i * half + r : i * half + r + 1, t * LANES : (t + 1) * LANES]
                out_ref[i, :, pl.ds((r * tiles + t) * LANES, LANES)] = piece


def route_kernel(slots, rank, place, counts, got_ref, out_ref, total_ref):
    owners, rows, _ = out_ref.shape
    width = total_ref.shape[1]
    tiles = width // LANES
    half = got_ref.shape[2] // width
    section = place[0]
    offset = jnp.int32(0)
    for s in range(owners):
        offset = offset + jnp.where(s < section, counts[s], 0)
    live = counts[section]
    flat = jnp.sum(got_ref[...], axis=0)
    total_ref[...] = jnp.zeros_like(total_ref)
    for r in range(half):
        for t in range(tiles):
            at = (r * tiles + t) * LANES
            total_ref[pl.ds(r, 1), pl.ds(t * LANES, LANES)] = flat[:, at : at + LANES]
    lane = lax.broadcasted_iota(jnp.int32, (rows, width), 1)
    total = jnp.where((lane // rank) % slots < live, total_ref[...], 0.0)
    square = jnp.sum(total * total)
    last = lax.broadcasted_iota(jnp.int32, (rows, 2 * LANES), 0) == rows - 1
    out_ref[...] = jnp.broadcast_to(jnp.where(last, square, 0.0)[None], out_ref.shape)
    side = lax.broadcasted_iota(jnp.int32, (rows, LANES), 1) // rank
    depths = owners * DEPTHS_PER_OWNER
    for k in range(slots):
        depth = lax.rem(offset + k + depths // 2, depths)
        owner = depth // DEPTHS_PER_OWNER
        spot = depth - owner * DEPTHS_PER_OWNER

        @pl.when(k < live)
        def _():
            for h in range(2):
                block = h * slots + k
                tile = total[:, (block // 2) * LANES : (block // 2 + 1) * LANES]
                turned = pltpu.roll(tile, rank, 1)
                value = jnp.where(side == block % 2, tile, 0.0)
                moved = jnp.where(side != block % 2, turned, 0.0)
                at = (owner, slice(None), pl.ds(h * LANES, LANES))
                out_ref[at] = out_ref[at] + jnp.where(spot == block % 2, value, moved)


def own_kernel(got_ref, owned_ref, square_ref):
    total = jnp.sum(got_ref[...], axis=0)
    owned_ref[...] = total
    square = total[total.shape[0] - 1 :, :LANES]
    square_ref[...] = jnp.broadcast_to(square[None], square_ref.shape)


def clip_kernel(entries, owned_ref, squares_ref, out_ref):
    chunk, _, rank = out_ref.shape
    half = chunk // 2
    total = jnp.sum(squares_ref[...], axis=0)
    factor = jnp.minimum(1.0, 0.5 / jnp.sqrt(total / entries + 1e-06))
    factor = jnp.broadcast_to(factor, (half, LANES))
    for h in range(2):
        tile = owned_ref[pl.ds(0, half), pl.ds(h * LANES, LANES)] * factor
        turned = pltpu.roll(owned_ref[:, pl.ds(h * LANES, LANES)], rank, 1)[:half] * factor
        out_ref[pl.ds(half * h, half), 0, :] = tile[:, :rank]
        out_ref[pl.ds(half * h, half), 1, :] = turned[:, :rank]


def on_device(counts, activations, cotangents):
    _, slots, tokens, hidden = activations.shape
    rank = cotangents.shape[3]
    sections, far = lax.axis_size("section"), lax.axis_size("far")
    replicas = Y_PAIR * far * NEAR * CORES
    chunk = hidden // replicas
    width = 2 * slots * rank
    half = chunk // 2
    place = jnp.stack([lax.axis_index("section"), lax.axis_index("core")]).astype(jnp.int32)
    groups = Y_PAIR * NEAR
    rows = groups * far * half
    with jax.named_scope("partials"):
        keep, send = call(
            functools.partial(partial_kernel, chunk, far),
            [(rows, width)] * 2,
            [SMEM, VMEM, VMEM],
            [pltpu.VMEM((hidden, width), jnp.float32)],
        )(
            place,
            activations.reshape(slots * tokens, hidden),
            jnp.swapaxes(cotangents[0], 1, 2),
        )
    with jax.named_scope("core_sum"):
        got = lax.ppermute(send, "core", [(0, 1), (1, 0)])
        (blocks,) = call(core_sum_kernel, [(groups, far * half, width)], [VMEM] * 2)(keep, got)
    with jax.named_scope("near_sum"):
        blocks = lax.all_to_all(blocks, ("pair", "near"), 0, 0, tiled=True)
        (blocks,) = call(near_sum_kernel, [(far, 1, half * width)], [VMEM])(blocks)
    with jax.named_scope("far_sum"):
        blocks = lax.all_to_all(blocks, "far", 0, 0, tiled=True)
    with jax.named_scope("route"):
        (routed,) = call(
            functools.partial(route_kernel, slots, rank),
            [(sections, PAD_ROWS, 2 * LANES)],
            [SMEM, SMEM, VMEM],
            [pltpu.VMEM((PAD_ROWS, width), jnp.float32)],
        )(place, counts, blocks)
        routed = lax.all_to_all(routed, "section", 0, 0, tiled=True)
        owned, squares = call(
            own_kernel, [(PAD_ROWS, 2 * LANES), (replicas, 1, LANES)], [VMEM]
        )(routed)
    with jax.named_scope("norm"):
        squares = lax.all_to_all(squares, ("pair", "far", "near", "core"), 0, 0, tiled=True)
    with jax.named_scope("clip"):
        entries = sections * DEPTHS_PER_OWNER * hidden * rank
        (out,) = call(
            functools.partial(clip_kernel, entries),
            [(chunk, DEPTHS_PER_OWNER, rank)],
            [VMEM, VMEM],
        )(owned, squares)
    return jnp.swapaxes(out, 0, 1)


def solution(mesh):
    sections, replicas = mesh.devices.shape
    far = replicas // (Y_PAIR * NEAR * CORES)
    split = Mesh(
        mesh.devices.reshape(sections, Y_PAIR, far, NEAR, CORES),
        ("section", "pair", "far", "near", "core"),
    )
    dp = ("pair", "far", "near", "core")
    return jax.shard_map(
        on_device,
        mesh=split,
        in_specs=(P(), P("section", None, dp, None), P("section", None, dp, None)),
        out_specs=P("section", dp, None),
        check_vma=False,
    )
```

time: 112 us -> 98.4 us (0.88)
  waiting for transfers between devices: 11 us -> 1.75 us
  starting transfers between devices: 18 us -> 16.1 us
  blocking collectives: 75.4 us -> 74.2 us
    psum x1 -> x0, blocking collectives: 10.2 us -> none  [on_device(): square = lax.psum(square, 'core')]
    all_to_all x2 -> x3, blocking collectives: 45.9 us -> 55.9 us  [the longest x1 23.5 us: on_device(): lax.all_to_all(squares, ('pair', 'far', 'near', 'core'), 0, 0, tiled=True)]
    ppermute x2 -> x1, waiting for transfers between devices: 11 us -> 1.75 us  [on_device(): got = lax.ppermute(send, 'core', [(0, 1), (1, 0)])]
    ppermute x2 -> x1, starting transfers between devices: 18 us -> 16.1 us  [on_device(): got = lax.ppermute(send, 'core', [(0, 1), (1, 0)])]
    unnamed x5 -> x6, local copies, waits for them, and re-layouts: 2.26 us -> 2.14 us
  transfers between devices with their start and end apart: 2 -> 1, of which waited for: 2 -> 1; matrix products, arithmetic and copies ran while one was open for 0% -> 0% of each run, Pallas kernels for 0% -> 0%
where the time goes in v2:
time: 98.4 us; the launch traced here: 98.1 us
  blocking collectives  74.2 us (75%)
  starting transfers between devices  16.1 us (16%)
  Pallas kernels  3.81 us (4%)
  local copies, waits for them, and re-layouts  2.14 us (2%)
  waiting for transfers between devices  1.75 us (2%)
    all_to_all x1, blocking collectives, on_device(): lax.all_to_all(squares, ('pair', 'far', 'near', 'core'), 0, 0, tiled=True)  23.5 us
    all_to_all x1, blocking collectives, on_device(): blocks = lax.all_to_all(blocks, 'far', 0, 0, tiled=True)  20.1 us
    all_to_all x1, blocking collectives, on_device(): routed = lax.all_to_all(routed, 'section', 0, 0, tiled=True)  18.3 us
    ppermute x1, starting transfers between devices, on_device(): got = lax.ppermute(send, 'core', [(0, 1), (1, 0)])  16.1 us
    all_to_all x1, blocking collectives, on_device(): blocks = lax.all_to_all(blocks, ('pair', 'near'), 0, 0, tiled=True)  12.3 us
    unnamed x6, local copies, waits for them, and re-layouts  2.14 us
    pallas_call x1, Pallas kernels, on_device(): call(functools.partial(partial_kernel, chunk, far), [(rows, width)] * 2,...  2 us
  transfers between devices with their start and end apart: 1, of which 1 were waited for; matrix products, arithmetic and copies ran while one was open for 0% of the time, Pallas kernels for 0%

profile of v2, /device:TPU:1, one launch (start us, length us, event | category | flops | bytes accessed | tf_op | source)
XLA Modules:
  0.0 98.1 jit_solution(8630627964279091514)
XLA Ops:
  0.0 0.1 pad_add_fusion.place
  0.1 0.0 copy-start
  0.1 1.3 %copy-done = bf16[1,3,128,1792]{3,2,1,0:T(8,128)(2,1)S(1)} copy-done((bf16[1,3,128,1792]{3,2,1,0:T(8,128)(2,1)S(1)}, bf16[1,3,128,1792]{3,2,1,0:T(8,128)(2,1)}, u32[]{:S(2)}) %copy-start) | copy-done | bytes 1376280
  1.4 0.0 copy-start.1
  1.4 0.8 copy-done.1
  2.2 2.0 %partials.1 = (f32[448,384]{1,0:T(8,128)S(1)}, f32[448,384]{1,0:T(8,128)S(1)}) custom-call(s32[2]{0:T(128)S(1)} %pad_add_fusion.place, bf16[384,1792]{1,0:T(8,128)(2,1)S(1)} %bitcast.7, bf16[3,64,128]{2,1,0:T(8,128)(2,1)S(1)} %bitcast.8), custom_call_target="tpu_custom_call" | custom-call | tf_op jit(solution)/shard_map/partials/pallas_call | solution.py:166
  4.2 16.1 %collective-permute-start = (f32[448,384]{1,0:T(8,128)S(1)}, f32[448,384]{1,0:T(8,128)S(1)}, u32[]{:S(2)}, u32[]{:S(2)}) collective-permute-start(f32[448,384]{1,0:T(8,128)S(1)} %get-tuple-element.10), channel_id=1, source_target_pairs={{0,1},{1,0},{2,3},{3,2},{4,5},{5,4},{6,7},{7,6},{8,9},{9,8},{10,11... | collective-permute-start | bytes 2064392 | tf_op jit(solution)/shard_map/core_sum/ppermute | solution.py:177
  20.3 1.7 %collective-permute-done.got_ref = f32[448,384]{1,0:T(8,128)S(1)} collective-permute-done((f32[448,384]{1,0:T(8,128)S(1)}, f32[448,384]{1,0:T(8,128)S(1)}, u32[]{:S(2)}, u32[]{:S(2)}) %collective-permute-start) | collective-permute-done | bytes 688160 | tf_op jit(solution)/shard_map/core_sum/ppermute | solution.py:177
  22.0 0.1 core_sum.1
  22.1 0.0 copy-start.2
  22.1 12.3 %all_to_all.20.got_ref = f32[4,112,384]{2,1,0:T(8,128)S(1)} all-to-all(f32[4,112,384]{2,1,0:T(8,128)S(1)} %core_sum.1), channel_id=1, replica_groups=mesh['section'=16,'pair'=2,'far'=8,'near'=2,'core'=2] {'pair','near'}, dimensions={0} | all-to-all | bytes 1376256 | tf_op jit(solution)/shard_map/near_sum/all_to_all | solution.py:180
  34.4 0.1 near_sum.1
  34.5 20.1 %all_to_all.21.got_ref = f32[8,1,5376]{2,1,0:T(1,128)S(1)} all-to-all(f32[8,1,5376]{2,1,0:T(1,128)S(1)} %near_sum.1), channel_id=1, replica_groups=mesh['section'=16,'pair'=2,'far'=8,'near'=2,'core'=2] {'far'}, dimensions={0} | all-to-all | bytes 344064 | tf_op jit(solution)/shard_map/far_sum/all_to_all | solution.py:183
  54.6 0.0 copy-done.2
  54.6 0.9 route.2
  55.5 18.3 %all_to_all.22.got_ref = f32[16,16,256]{2,1,0:T(8,128)S(1)} all-to-all(f32[16,16,256]{2,1,0:T(8,128)S(1)} %route.2), channel_id=1, replica_groups=mesh['section'=16,'pair'=2,'far'=8,'near'=2,'core'=2] {'section'}, dimensions={0} | all-to-all | bytes 524288 | tf_op jit(solution)/shard_map/route/all_to_all | solution.py:191
  73.8 23.5 %all_to_all.23.squares_ref = f32[64,1,128]{2,1,0:T(1,128)S(1)} all-to-all(f32[64,1,128]{2,1,0:T(1,128)S(1)} %get-tuple-element.12), channel_id=1, replica_groups=mesh['section'=16,'pair'=2,'far'=8,'near'=2,'core'=2] {'pair','far','nea..., dimensions={0} | all-to-all | bytes 65536 | tf_op jit(solution)/shard_map/norm/all_to_all | solution.py:196
  97.3 0.7 clip.1
  (1 shorter events, 0.0 us)
Async XLA Ops:
  0.1 1.3 %copy-start = (bf16[1,3,128,1792]{3,2,1,0:T(8,128)(2,1)S(1)}, bf16[1,3,128,1792]{3,2,1,0:T(8,128)(2,1)}, u32[]{:S(2)}) copy-start(bf16[1,3,128,1792]{3,2,1,0:T(8,128)(2,1)} %param.4) | copy-start | bytes 4128772
  1.4 0.8 copy-start.1
  4.2 17.8 %collective-permute-start = (f32[448,384]{1,0:T(8,128)S(1)}, f32[448,384]{1,0:T(8,128)S(1)}, u32[]{:S(2)}, u32[]{:S(2)}) collective-permute-start(f32[448,384]{1,0:T(8,128)S(1)} %get-tuple-element.10), channel_id=1, source_target_pairs={{0,1},{1,0},{2,3},{3,2},{4,5},{5,4},{6,7},{7,6},{8,9},{9,8},{10,11... | collective-permute-start | bytes 2064392 | tf_op jit(solution)/shard_map/core_sum/ppermute | solution.py:177
  22.1 32.5 %copy-start.2 = (s32[16]{0:T(128)S(1)}, s32[16]{0:T(128)}, u32[]{:S(2)}) copy-start(s32[16]{0:T(128)} %counts.1) | copy-start | bytes 196

commit v3 on v2

v3 whole, which is shorter than its diff:
```python
import functools

import jax
import jax.numpy as jnp
from jax import lax
from jax.experimental import pallas as pl
from jax.experimental.pallas import tpu as pltpu
from jax.sharding import Mesh, PartitionSpec as P

DEPTHS_PER_OWNER = 2
Y_PAIR = 2
NEAR = 2
CORES = 2
LANES = 128
PAD_ROWS = 16
TILES = 3
OVER_ROWS = (((0,), (0,)), ((), ()))
VMEM = pl.BlockSpec(memory_space=pltpu.VMEM)
SMEM = pl.BlockSpec(memory_space=pltpu.SMEM)


def call(body, shapes, in_specs, scratch=(), dtype=jnp.float32, cost=None):
    return pl.pallas_call(
        body,
        out_shape=tuple(jax.ShapeDtypeStruct(s, dtype) for s in shapes),
        in_specs=in_specs,
        out_specs=tuple(VMEM for _ in shapes),
        scratch_shapes=list(scratch),
        cost_estimate=cost,
        compiler_params=pltpu.CompilerParams(vmem_limit_bytes=24 * 1024 * 1024),
    )


def spread_kernel(c_ref, blocks_ref):
    slots, rank, tokens = c_ref.shape
    width = blocks_ref.shape[1]
    lane = lax.broadcasted_iota(jnp.int32, (rank, width), 1)
    row = lax.broadcasted_iota(jnp.int32, (rank, width), 0)
    spread = (lane % rank == row).astype(jnp.bfloat16)
    slot = jnp.minimum(lax.broadcasted_iota(jnp.int32, (tokens, width), 1) // rank, slots - 1)
    for k in range(slots):
        tiled = lax.dot_general(c_ref[k], spread, OVER_ROWS, preferred_element_type=jnp.float32)
        blocks_ref[pl.ds(k * tokens, tokens), :] = jnp.where(slot == k, tiled, 0.0).astype(jnp.bfloat16)


def partial_kernel(chunk, far, a_ref, blocks_ref, keep_ref, send_ref, p_ref):
    sums = lax.dot_general(a_ref[...], blocks_ref[...], OVER_ROWS, preferred_element_type=jnp.float32)
    for t in range(2):
        p_ref[t] = sums[:, t * LANES : (t + 1) * LANES]
    half = chunk // 2
    left = lax.broadcasted_iota(jnp.int32, (half, LANES), 1) < LANES // 2

    def pack(core, out_ref):
        for pair in range(Y_PAIR):
            for near in range(NEAR):
                for step in range(far):
                    start = (((pair * far + step) * NEAR + near) * CORES + core) * chunk
                    upper, lower = pl.ds(start, half), pl.ds(start + half, half)
                    tiles = (
                        p_ref[0, upper, :],
                        jnp.where(left, p_ref[1, upper, :], p_ref[1, lower, :]),
                        p_ref[0, lower, :],
                    )
                    for t in range(TILES):
                        at = pl.ds((t * far + step) * half, half)
                        out_ref[pair * NEAR + near, at, :] = tiles[t]

    core = lax.axis_index("core")

    @pl.when(core == 0)
    def _():
        pack(1, send_ref)
        pack(0, keep_ref)

    @pl.when(core == 1)
    def _():
        pack(0, send_ref)
        pack(1, keep_ref)


def core_sum_kernel(mask_ref, keep_ref, got_ref, out_ref):
    del mask_ref
    out_ref[...] = keep_ref[...] + got_ref[...]


def near_sum_kernel(got_ref, out_ref):
    total = jnp.sum(got_ref[...], axis=0)
    far = out_ref.shape[0]
    half = total.shape[0] // (TILES * far)
    for i in range(far):
        for t in range(TILES):
            for r in range(half):
                row = (t * far + i) * half + r
                out_ref[i, :, pl.ds((t * half + r) * LANES, LANES)] = total[row : row + 1, :]


def mask_kernel(slots, rank, counts, mask_ref):
    owners = counts.shape[0]
    section = lax.axis_index("section")
    offset = jnp.int32(0)
    for s in range(owners):
        offset = offset + jnp.where(s < section, counts[s], 0)
    live = counts[section]
    row = lax.broadcasted_iota(jnp.int32, mask_ref.shape, 0)
    side = lax.broadcasted_iota(jnp.int32, mask_ref.shape, 1) // rank
    depths = owners * DEPTHS_PER_OWNER
    mask = jnp.zeros(mask_ref.shape, jnp.bool_)
    for k in range(slots):
        depth = lax.rem(offset + k + depths // 2, depths)
        owner = depth // DEPTHS_PER_OWNER
        spot = depth - owner * DEPTHS_PER_OWNER
        mask = mask | ((row == owner * slots + k) & (side == spot) & (k < live))
    base = owners * slots
    mask = mask | ((row == base) & (side < live)) | ((row == base + 1) & (slots - 1 < live))
    mask_ref[...] = mask.astype(jnp.float32)


def route_kernel(slots, mask_ref, got_ref, out_ref, total_ref):
    owners, rows, _ = out_ref.shape
    half = got_ref.shape[2] // (TILES * LANES)
    flat = jnp.sum(got_ref[...], axis=0)
    total_ref[...] = jnp.zeros_like(total_ref)
    for t in range(TILES):
        for r in range(half):
            at = (t * half + r) * LANES
            total_ref[t, pl.ds(r, 1), :] = flat[:, at : at + LANES]
    base = owners * slots
    first, last = mask_ref[pl.ds(base, 1), :], mask_ref[pl.ds(base + 1, 1), :]
    live = (first, last, first)
    tiles = [total_ref[t] * live[t] for t in range(TILES)]
    squares = jnp.sum(sum(x * x for x in tiles), axis=0, keepdims=True)
    left = lax.broadcasted_iota(jnp.int32, (rows, LANES), 1) < LANES // 2
    turned = [pltpu.roll(x, LANES // 2, 1) for x in tiles]
    both = [jnp.where(left, x, y) for x, y in zip(tiles, turned)]
    flip = [jnp.where(left, y, x) for x, y in zip(tiles, turned)]
    halves = ((both[0], flip[0], both[1]), (both[2], flip[2], flip[1]))
    bottom = lax.broadcasted_iota(jnp.int32, (rows, LANES), 0) == rows - 1
    blank = jnp.where(bottom, squares, 0.0)
    for e in range(owners):
        for h in range(2):
            value = blank
            for k in range(slots):
                value = value + mask_ref[pl.ds(e * slots + k, 1), :] * halves[h][k]
            out_ref[e, :, pl.ds(h * LANES, LANES)] = value


def own_kernel(got_ref, owned_ref, square_ref):
    total = jnp.sum(got_ref[...], axis=0)
    owned_ref[...] = total
    square = total[total.shape[0] - 1 :, :LANES]
    square_ref[...] = jnp.broadcast_to(square[None], square_ref.shape)


def clip_kernel(entries, owned_ref, squares_ref, out_ref):
    chunk, _, rank = out_ref.shape
    half = chunk // 2
    total = jnp.sum(jnp.sum(squares_ref[...], axis=0), axis=1, keepdims=True)
    factor = jnp.minimum(1.0, 0.5 / jnp.sqrt(total / entries + 1e-06))
    factor = jnp.broadcast_to(factor, (half, LANES))
    for h in range(2):
        tile = owned_ref[pl.ds(0, half), pl.ds(h * LANES, LANES)] * factor
        turned = pltpu.roll(owned_ref[:, pl.ds(h * LANES, LANES)], rank, 1)[:half] * factor
        out_ref[pl.ds(half * h, half), 0, :] = tile[:, :rank]
        out_ref[pl.ds(half * h, half), 1, :] = turned[:, :rank]


def on_device(counts, activations, cotangents):
    _, slots, tokens, hidden = activations.shape
    rank = cotangents.shape[3]
    sections, far = lax.axis_size("section"), lax.axis_size("far")
    replicas = Y_PAIR * far * NEAR * CORES
    chunk = hidden // replicas
    half = chunk // 2
    groups = Y_PAIR * NEAR
    packed = (groups, TILES * far * half, LANES)
    with jax.named_scope("partials"):
        (blocks,) = call(
            spread_kernel,
            [(slots * tokens, 2 * LANES)],
            [VMEM],
            dtype=jnp.bfloat16,
            cost=pl.CostEstimate(flops=4 * 10**9, bytes_accessed=10**6, transcendentals=0),
        )(jnp.swapaxes(cotangents[0], 1, 2))
        keep, send = call(
            functools.partial(partial_kernel, chunk, far),
            [packed] * 2,
            [VMEM, VMEM],
            [pltpu.VMEM((2, hidden, LANES), jnp.float32)],
        )(activations.reshape(slots * tokens, hidden), blocks)
    with jax.named_scope("core_sum"):
        got = lax.ppermute(send, "core", [(0, 1), (1, 0)])
        (mask,) = call(
            functools.partial(mask_kernel, slots, rank), [(sections * slots + 8, LANES)], [SMEM]
        )(counts)
        (blocks,) = call(core_sum_kernel, [packed], [VMEM] * 3)(mask, keep, got)
    with jax.named_scope("near_sum"):
        blocks = lax.all_to_all(blocks, ("pair", "near"), 0, 0, tiled=True)
        (blocks,) = call(near_sum_kernel, [(far, 1, TILES * half * LANES)], [VMEM])(blocks)
    with jax.named_scope("far_sum"):
        blocks = lax.all_to_all(blocks, "far", 0, 0, tiled=True)
    with jax.named_scope("route"):
        (routed,) = call(
            functools.partial(route_kernel, slots),
            [(sections, PAD_ROWS, 2 * LANES)],
            [VMEM, VMEM],
            [pltpu.VMEM((TILES, PAD_ROWS, LANES), jnp.float32)],
        )(mask, blocks)
        routed = lax.all_to_all(routed, "section", 0, 0, tiled=True)
        owned, squares = call(
            own_kernel, [(PAD_ROWS, 2 * LANES), (replicas, 1, LANES)], [VMEM]
        )(routed)
    with jax.named_scope("norm"):
        squares = lax.all_to_all(squares, ("pair", "far", "near", "core"), 0, 0, tiled=True)
    with jax.named_scope("clip"):
        entries = sections * DEPTHS_PER_OWNER * hidden * rank
        (out,) = call(
            functools.partial(clip_kernel, entries),
            [(chunk, DEPTHS_PER_OWNER, rank)],
            [VMEM, VMEM],
        )(owned, squares)
    return jnp.swapaxes(out, 0, 1)


def solution(mesh):
    sections, replicas = mesh.devices.shape
    far = replicas // (Y_PAIR * NEAR * CORES)
    split = Mesh(
        mesh.devices.reshape(sections, Y_PAIR, far, NEAR, CORES),
        ("section", "pair", "far", "near", "core"),
    )
    dp = ("pair", "far", "near", "core")
    return jax.shard_map(
        on_device,
        mesh=split,
        in_specs=(P(), P("section", None, dp, None), P("section", None, dp, None)),
        out_specs=P("section", dp, None),
        check_vma=False,
    )
```

time: 98.4 us -> 96.5 us (0.981)
    pallas_call x4 -> x6, Pallas kernels: 3.06 us -> 2.04 us  [the longest x1 0.8 us: on_device(): call(functools.partial(partial_kernel, chunk, far), [packed] * 2, [VMEM,...]
  transfers between devices with their start and end apart: 1 -> 1, of which waited for: 1 -> 1; matrix products, arithmetic and copies ran while one was open for 0% -> 0% of each run, Pallas kernels for 0% -> 1%
where the time goes in v3:
time: 96.5 us; the launch traced here: 96.2 us
  blocking collectives  74.2 us (77%)
  starting transfers between devices  16 us (17%)
  Pallas kernels  2.86 us (3%)
  local copies, waits for them, and re-layouts  1.88 us (2%)
  waiting for transfers between devices  1.12 us (1%)
    all_to_all x1, blocking collectives, on_device(): lax.all_to_all(squares, ('pair', 'far', 'near', 'core'), 0, 0, tiled=True)  23.5 us
    all_to_all x1, blocking collectives, on_device(): blocks = lax.all_to_all(blocks, 'far', 0, 0, tiled=True)  20.1 us
    all_to_all x1, blocking collectives, on_device(): routed = lax.all_to_all(routed, 'section', 0, 0, tiled=True)  18.3 us
    ppermute x1, starting transfers between devices, on_device(): got = lax.ppermute(send, 'core', [(0, 1), (1, 0)])  16 us
    all_to_all x1, blocking collectives, on_device(): blocks = lax.all_to_all(blocks, ('pair', 'near'), 0, 0, tiled=True)  12.3 us
  transfers between devices with their start and end apart: 1, of which 1 were waited for; matrix products, arithmetic and copies ran while one was open for 0% of the time, Pallas kernels for 1%

profile of v3, /device:TPU:1, one launch (start us, length us, event | category | flops | bytes accessed | tf_op | source)
XLA Modules:
  0.0 96.2 jit_solution(9405301417191127048)
XLA Ops:
  0.0 0.0 copy-start.2
  0.0 0.8 copy-done.2
  0.8 0.0 copy-start
  0.8 0.2 partials.2.blocks_ref
  1.0 0.0 copy-start.1
  1.1 1.1 %copy-done = bf16[1,3,128,1792]{3,2,1,0:T(8,128)(2,1)S(1)} copy-done((bf16[1,3,128,1792]{3,2,1,0:T(8,128)(2,1)S(1)}, bf16[1,3,128,1792]{3,2,1,0:T(8,128)(2,1)}, u32[]{:S(2)}) %copy-start) | copy-done | bytes 1376280
  2.1 0.8 partials.3
  2.9 16.0 %collective-permute-start = (f32[4,336,128]{2,1,0:T(8,128)S(1)}, f32[4,336,128]{2,1,0:T(8,128)S(1)}, u32[]{:S(2)}, u32[]{:S(2)}) collective-permute-start(f32[4,336,128]{2,1,0:T(8,128)S(1)} %get-tuple-element.10), channel_id=1, source_target_pairs={{0,1},{1,0},{2,3},{3,2},{4,5},{5,4},{6,7},{7,6},{8,9},{9,8},{10,11... | collective-permute-start | bytes 2064392 | tf_op jit(solution)/shard_map/core_sum/ppermute | solution.py:191
  19.0 0.0 copy-done.1
  19.0 0.6 core_sum.2.mask_ref
  19.6 1.1 %collective-permute-done.got_ref = f32[4,336,128]{2,1,0:T(8,128)S(1)} collective-permute-done((f32[4,336,128]{2,1,0:T(8,128)S(1)}, f32[4,336,128]{2,1,0:T(8,128)S(1)}, u32[]{:S(2)}, u32[]{:S(2)}) %collective-permute-start) | collective-permute-done | bytes 688160 | tf_op jit(solution)/shard_map/core_sum/ppermute | solution.py:191
  20.8 0.1 core_sum.3
  20.8 12.3 %all_to_all.20.got_ref = f32[4,336,128]{2,1,0:T(8,128)S(1)} all-to-all(f32[4,336,128]{2,1,0:T(8,128)S(1)} %core_sum.3), channel_id=1, replica_groups=mesh['section'=16,'pair'=2,'far'=8,'near'=2,'core'=2] {'pair','near'}, dimensions={0} | all-to-all | bytes 1376256 | tf_op jit(solution)/shard_map/near_sum/all_to_all | solution.py:197
  33.1 0.1 near_sum.1
  33.2 20.1 %all_to_all.21.got_ref = f32[8,1,5376]{2,1,0:T(1,128)S(1)} all-to-all(f32[8,1,5376]{2,1,0:T(1,128)S(1)} %near_sum.1), channel_id=1, replica_groups=mesh['section'=16,'pair'=2,'far'=8,'near'=2,'core'=2] {'far'}, dimensions={0} | all-to-all | bytes 344064 | tf_op jit(solution)/shard_map/far_sum/all_to_all | solution.py:200
  53.3 0.2 route.2
  53.5 18.3 %all_to_all.22.got_ref = f32[16,16,256]{2,1,0:T(8,128)S(1)} all-to-all(f32[16,16,256]{2,1,0:T(8,128)S(1)} %route.2), channel_id=1, replica_groups=mesh['section'=16,'pair'=2,'far'=8,'near'=2,'core'=2] {'section'}, dimensions={0} | all-to-all | bytes 524288 | tf_op jit(solution)/shard_map/route/all_to_all | solution.py:208
  71.9 23.5 %all_to_all.23.squares_ref = f32[64,1,128]{2,1,0:T(1,128)S(1)} all-to-all(f32[64,1,128]{2,1,0:T(1,128)S(1)} %get-tuple-element.12), channel_id=1, replica_groups=mesh['section'=16,'pair'=2,'far'=8,'near'=2,'core'=2] {'pair','far','nea..., dimensions={0} | all-to-all | bytes 65536 | tf_op jit(solution)/shard_map/norm/all_to_all | solution.py:213
  95.4 0.8 clip.1
  (1 shorter events, 0.0 us)
Async XLA Ops:
  0.0 0.8 copy-start.2
  0.8 1.3 %copy-start = (bf16[1,3,128,1792]{3,2,1,0:T(8,128)(2,1)S(1)}, bf16[1,3,128,1792]{3,2,1,0:T(8,128)(2,1)}, u32[]{:S(2)}) copy-start(bf16[1,3,128,1792]{3,2,1,0:T(8,128)(2,1)} %param.4) | copy-start | bytes 4128772
  1.0 18.0 %copy-start.1 = (s32[16]{0:T(128)S(1)}, s32[16]{0:T(128)}, u32[]{:S(2)}) copy-start(s32[16]{0:T(128)} %counts.1) | copy-start | bytes 196
  2.9 17.8 %collective-permute-start = (f32[4,336,128]{2,1,0:T(8,128)S(1)}, f32[4,336,128]{2,1,0:T(8,128)S(1)}, u32[]{:S(2)}, u32[]{:S(2)}) collective-permute-start(f32[4,336,128]{2,1,0:T(8,128)S(1)} %get-tuple-element.10), channel_id=1, source_target_pairs={{0,1},{1,0},{2,3},{3,2},{4,5},{5,4},{6,7},{7,6},{8,9},{9,8},{10,11... | collective-permute-start | bytes 2064392 | tf_op jit(solution)/shard_map/core_sum/ppermute | solution.py:191

commit v4 on v3

--- a/solution.py
+++ b/solution.py
@@ -31,15 +31,21 @@
     )
 
 
-def spread_kernel(c_ref, blocks_ref):
+def spread_kernel(spread_ref):
+    rank, width = spread_ref.shape
+    lane = lax.broadcasted_iota(jnp.int32, (rank, width), 1)
+    row = lax.broadcasted_iota(jnp.int32, (rank, width), 0)
+    spread_ref[...] = (lane % rank == row).astype(jnp.bfloat16)
+
+
+def blocks_kernel(spread_ref, c_ref, blocks_ref):
     slots, rank, tokens = c_ref.shape
     width = blocks_ref.shape[1]
-    lane = lax.broadcasted_iota(jnp.int32, (rank, width), 1)
-    row = lax.broadcasted_iota(jnp.int32, (rank, width), 0)
-    spread = (lane % rank == row).astype(jnp.bfloat16)
     slot = jnp.minimum(lax.broadcasted_iota(jnp.int32, (tokens, width), 1) // rank, slots - 1)
     for k in range(slots):
-        tiled = lax.dot_general(c_ref[k], spread, OVER_ROWS, preferred_element_type=jnp.float32)
+        tiled = lax.dot_general(
+            c_ref[k], spread_ref[...], OVER_ROWS, preferred_element_type=jnp.float32
+        )
         blocks_ref[pl.ds(k * tokens, tokens), :] = jnp.where(slot == k, tiled, 0.0).astype(jnp.bfloat16)
 
 
@@ -83,14 +89,14 @@
     out_ref[...] = keep_ref[...] + got_ref[...]
 
 
-def near_sum_kernel(got_ref, out_ref):
+def near_sum_kernel(order, got_ref, out_ref):
     total = jnp.sum(got_ref[...], axis=0)
     far = out_ref.shape[0]
     half = total.shape[0] // (TILES * far)
     for i in range(far):
         for t in range(TILES):
             for r in range(half):
-                row = (t * far + i) * half + r
+                row = (t * far + order[i]) * half + r
                 out_ref[i, :, pl.ds((t * half + r) * LANES, LANES)] = total[row : row + 1, :]
 
 
@@ -172,15 +178,17 @@
     chunk = hidden // replicas
     half = chunk // 2
     groups = Y_PAIR * NEAR
+    order = sorted(range(far), key=lambda i: (i % 2, i % (far // 2)))
     packed = (groups, TILES * far * half, LANES)
     with jax.named_scope("partials"):
+        hint = pl.CostEstimate(flops=4 * 10**9, bytes_accessed=10**6, transcendentals=0)
+        (spread,) = call(spread_kernel, [(rank, 2 * LANES)], [], dtype=jnp.bfloat16, cost=hint)()
         (blocks,) = call(
-            spread_kernel,
+            blocks_kernel,
             [(slots * tokens, 2 * LANES)],
-            [VMEM],
+            [VMEM, VMEM],
             dtype=jnp.bfloat16,
-            cost=pl.CostEstimate(flops=4 * 10**9, bytes_accessed=10**6, transcendentals=0),
-        )(jnp.swapaxes(cotangents[0], 1, 2))
+        )(spread, jnp.swapaxes(cotangents[0], 1, 2))
         keep, send = call(
             functools.partial(partial_kernel, chunk, far),
             [packed] * 2,
@@ -195,9 +203,13 @@
         (blocks,) = call(core_sum_kernel, [packed], [VMEM] * 3)(mask, keep, got)
     with jax.named_scope("near_sum"):
         blocks = lax.all_to_all(blocks, ("pair", "near"), 0, 0, tiled=True)
-        (blocks,) = call(near_sum_kernel, [(far, 1, TILES * half * LANES)], [VMEM])(blocks)
+        (blocks,) = call(
+            functools.partial(near_sum_kernel, order), [(far, 1, TILES * half * LANES)], [VMEM]
+        )(blocks)
     with jax.named_scope("far_sum"):
-        blocks = lax.all_to_all(blocks, "far", 0, 0, tiled=True)
+        blocks = lax.all_to_all(
+            blocks, "far", 0, 0, axis_index_groups=[order], tiled=True
+        )
     with jax.named_scope("route"):
         (routed,) = call(
             functools.partial(route_kernel, slots),

time: 96.5 us -> 96.5 us (level)
    all_to_all x1, blocking collectives: 23.5 us -> 26.1 us  [on_device(): lax.all_to_all(squares, ('pair', 'far', 'near', 'core'), 0, 0, tiled=True)]
    all_to_all x1, blocking collectives: 20.1 us -> 18.4 us  [on_device(): lax.all_to_all(blocks, 'far', 0, 0, axis_index_groups=[order], tiled=True)]
where the time goes in v4:
time: 96.5 us; the launch traced here: 96.2 us
  blocking collectives  75 us (78%)
  starting transfers between devices  16 us (17%)
  Pallas kernels  2.87 us (3%)
  waiting for transfers between devices  1.12 us (1%)
  local copies, waits for them, and re-layouts  1.11 us (1%)
    all_to_all x1, blocking collectives, on_device(): lax.all_to_all(squares, ('pair', 'far', 'near', 'core'), 0, 0, tiled=True)  26.1 us
    all_to_all x1, blocking collectives, on_device(): lax.all_to_all(blocks, 'far', 0, 0, axis_index_groups=[order], tiled=True)  18.4 us
    all_to_all x1, blocking collectives, on_device(): routed = lax.all_to_all(routed, 'section', 0, 0, tiled=True)  18.2 us
    ppermute x1, starting transfers between devices, on_device(): got = lax.ppermute(send, 'core', [(0, 1), (1, 0)])  16 us
    all_to_all x1, blocking collectives, on_device(): blocks = lax.all_to_all(blocks, ('pair', 'near'), 0, 0, tiled=True)  12.3 us
  transfers between devices with their start and end apart: 1, of which 1 were waited for; matrix products, arithmetic and copies ran while one was open for 0% of the time, Pallas kernels for 1%

profile of v4, /device:TPU:1, one launch (start us, length us, event | category | flops | bytes accessed | tf_op | source)
XLA Modules:
  0.0 96.2 jit_solution(17812681972347582614)
XLA Ops:
  0.0 0.0 copy-start.1
  0.0 0.0 copy-start
  0.0 0.0 copy-start.2
  0.0 0.8 copy-done.1
  0.8 0.2 partials.4.blocks_ref
  1.0 0.3 copy-done
  1.4 0.8 partials.5
  2.2 16.0 %collective-permute-start = (f32[4,336,128]{2,1,0:T(8,128)S(1)}, f32[4,336,128]{2,1,0:T(8,128)S(1)}, u32[]{:S(2)}, u32[]{:S(2)}) collective-permute-start(f32[4,336,128]{2,1,0:T(8,128)S(1)} %get-tuple-element.10), channel_id=1, source_target_pairs={{0,1},{1,0},{2,3},{3,2},{4,5},{5,4},{6,7},{7,6},{8,9},{9,8},{10,11... | collective-permute-start | bytes 2064392 | tf_op jit(solution)/shard_map/core_sum/ppermute | solution.py:199
  18.2 0.0 copy-done.2
  18.2 0.6 core_sum.2.mask_ref
  18.9 1.1 %collective-permute-done.got_ref = f32[4,336,128]{2,1,0:T(8,128)S(1)} collective-permute-done((f32[4,336,128]{2,1,0:T(8,128)S(1)}, f32[4,336,128]{2,1,0:T(8,128)S(1)}, u32[]{:S(2)}, u32[]{:S(2)}) %collective-permute-start) | collective-permute-done | bytes 688160 | tf_op jit(solution)/shard_map/core_sum/ppermute | solution.py:199
  20.0 0.1 core_sum.3
  20.1 12.3 %all_to_all.20.got_ref = f32[4,336,128]{2,1,0:T(8,128)S(1)} all-to-all(f32[4,336,128]{2,1,0:T(8,128)S(1)} %core_sum.3), channel_id=1, replica_groups=mesh['section'=16,'pair'=2,'far'=8,'near'=2,'core'=2] {'pair','near'}, dimensions={0} | all-to-all | bytes 1376256 | tf_op jit(solution)/shard_map/near_sum/all_to_all | solution.py:205
  32.3 0.1 near_sum.1
  32.5 18.4 %all_to_all.21.got_ref = f32[8,1,5376]{2,1,0:T(1,128)S(1)} all-to-all(f32[8,1,5376]{2,1,0:T(1,128)S(1)} %near_sum.1), channel_id=1, replica_groups={{0,16,8,24,4,20,12,28},{1,17,9,25,5,21,13,29},{2,18,10,26,6,22,14,30},{..., dimensions={0} | all-to-all | bytes 344064 | tf_op jit(solution)/shard_map/far_sum/all_to_all | solution.py:210
  50.8 0.2 route.2
  51.1 18.2 %all_to_all.22.got_ref = f32[16,16,256]{2,1,0:T(8,128)S(1)} all-to-all(f32[16,16,256]{2,1,0:T(8,128)S(1)} %route.2), channel_id=1, replica_groups=mesh['section'=16,'pair'=2,'far'=8,'near'=2,'core'=2] {'section'}, dimensions={0} | all-to-all | bytes 524288 | tf_op jit(solution)/shard_map/route/all_to_all | solution.py:220
  69.3 26.1 %all_to_all.23.squares_ref = f32[64,1,128]{2,1,0:T(1,128)S(1)} all-to-all(f32[64,1,128]{2,1,0:T(1,128)S(1)} %get-tuple-element.12), channel_id=1, replica_groups=mesh['section'=16,'pair'=2,'far'=8,'near'=2,'core'=2] {'pair','far','nea..., dimensions={0} | all-to-all | bytes 65536 | tf_op jit(solution)/shard_map/norm/all_to_all | solution.py:225
  95.4 0.8 clip.1
  (2 shorter events, 0.0 us)
Async XLA Ops:
  0.0 0.8 copy-start.1
  0.0 1.4 %copy-start = (bf16[1,3,128,1792]{3,2,1,0:T(8,128)(2,1)S(1)}, bf16[1,3,128,1792]{3,2,1,0:T(8,128)(2,1)}, u32[]{:S(2)}) copy-start(bf16[1,3,128,1792]{3,2,1,0:T(8,128)(2,1)} %param.4) | copy-start | bytes 4128772
  0.0 18.2 %copy-start.2 = (s32[16]{0:T(128)S(1)}, s32[16]{0:T(128)}, u32[]{:S(2)}) copy-start(s32[16]{0:T(128)} %counts.1) | copy-start | bytes 196
  2.2 17.8 %collective-permute-start = (f32[4,336,128]{2,1,0:T(8,128)S(1)}, f32[4,336,128]{2,1,0:T(8,128)S(1)}, u32[]{:S(2)}, u32[]{:S(2)}) collective-permute-start(f32[4,336,128]{2,1,0:T(8,128)S(1)} %get-tuple-element.10), channel_id=1, source_target_pairs={{0,1},{1,0},{2,3},{3,2},{4,5},{5,4},{6,7},{7,6},{8,9},{9,8},{10,11... | collective-permute-start | bytes 2064392 | tf_op jit(solution)/shard_map/core_sum/ppermute | solution.py:199

commit v5 on v4

--- a/solution.py
+++ b/solution.py
@@ -69,7 +69,7 @@
                     )
                     for t in range(TILES):
                         at = pl.ds((t * far + step) * half, half)
-                        out_ref[pair * NEAR + near, at, :] = tiles[t]
+                        out_ref[near * Y_PAIR + pair, at, :] = tiles[t]
 
     core = lax.axis_index("core")
 
@@ -89,14 +89,14 @@
     out_ref[...] = keep_ref[...] + got_ref[...]
 
 
-def near_sum_kernel(order, got_ref, out_ref):
+def near_sum_kernel(got_ref, out_ref):
     total = jnp.sum(got_ref[...], axis=0)
     far = out_ref.shape[0]
     half = total.shape[0] // (TILES * far)
     for i in range(far):
         for t in range(TILES):
             for r in range(half):
-                row = (t * far + order[i]) * half + r
+                row = (t * far + i) * half + r
                 out_ref[i, :, pl.ds((t * half + r) * LANES, LANES)] = total[row : row + 1, :]
 
 
@@ -121,8 +121,7 @@
     mask_ref[...] = mask.astype(jnp.float32)
 
 
-def route_kernel(slots, mask_ref, got_ref, out_ref, total_ref):
-    owners, rows, _ = out_ref.shape
+def square_kernel(base, mask_ref, got_ref, total_ref, square_ref):
     half = got_ref.shape[2] // (TILES * LANES)
     flat = jnp.sum(got_ref[...], axis=0)
     total_ref[...] = jnp.zeros_like(total_ref)
@@ -130,11 +129,23 @@
         for r in range(half):
             at = (t * half + r) * LANES
             total_ref[t, pl.ds(r, 1), :] = flat[:, at : at + LANES]
+    first, last = mask_ref[pl.ds(base, 1), :], mask_ref[pl.ds(base + 1, 1), :]
+    live = (first, last, first)
+    squares = jnp.zeros((total_ref.shape[1], LANES), jnp.float32)
+    for t in range(TILES):
+        x = total_ref[t] * live[t]
+        squares = squares + x * x
+    squares = jnp.sum(squares, axis=0, keepdims=True)
+    square_ref[...] = jnp.broadcast_to(squares[None], square_ref.shape)
+
+
+def route_kernel(slots, mask_ref, total_ref, squares_ref, out_ref):
+    owners, rows, _ = out_ref.shape
     base = owners * slots
     first, last = mask_ref[pl.ds(base, 1), :], mask_ref[pl.ds(base + 1, 1), :]
     live = (first, last, first)
     tiles = [total_ref[t] * live[t] for t in range(TILES)]
-    squares = jnp.sum(sum(x * x for x in tiles), axis=0, keepdims=True)
+    squares = jnp.sum(squares_ref[...], axis=0)
     left = lax.broadcasted_iota(jnp.int32, (rows, LANES), 1) < LANES // 2
     turned = [pltpu.roll(x, LANES // 2, 1) for x in tiles]
     both = [jnp.where(left, x, y) for x, y in zip(tiles, turned)]
@@ -150,24 +161,18 @@
             out_ref[e, :, pl.ds(h * LANES, LANES)] = value
 
 
-def own_kernel(got_ref, owned_ref, square_ref):
-    total = jnp.sum(got_ref[...], axis=0)
-    owned_ref[...] = total
-    square = total[total.shape[0] - 1 :, :LANES]
-    square_ref[...] = jnp.broadcast_to(square[None], square_ref.shape)
-
-
-def clip_kernel(entries, owned_ref, squares_ref, out_ref):
+def clip_kernel(entries, got_ref, out_ref):
     chunk, _, rank = out_ref.shape
     half = chunk // 2
-    total = jnp.sum(jnp.sum(squares_ref[...], axis=0), axis=1, keepdims=True)
-    factor = jnp.minimum(1.0, 0.5 / jnp.sqrt(total / entries + 1e-06))
-    factor = jnp.broadcast_to(factor, (half, LANES))
+    owned = jnp.sum(got_ref[...], axis=0)
+    square = jnp.sum(owned[owned.shape[0] - 1 :, :LANES], axis=1, keepdims=True)
+    factor = jnp.minimum(1.0, 0.5 / jnp.sqrt(square / entries + 1e-06))
+    owned = owned * jnp.broadcast_to(factor, owned.shape)
     for h in range(2):
-        tile = owned_ref[pl.ds(0, half), pl.ds(h * LANES, LANES)] * factor
-        turned = pltpu.roll(owned_ref[:, pl.ds(h * LANES, LANES)], rank, 1)[:half] * factor
-        out_ref[pl.ds(half * h, half), 0, :] = tile[:, :rank]
-        out_ref[pl.ds(half * h, half), 1, :] = turned[:, :rank]
+        tile = owned[:, h * LANES : (h + 1) * LANES]
+        turned = pltpu.roll(tile, rank, 1)
+        out_ref[pl.ds(half * h, half), 0, :] = tile[:half, :rank]
+        out_ref[pl.ds(half * h, half), 1, :] = turned[:half, :rank]
 
 
 def on_device(counts, activations, cotangents):
@@ -178,7 +183,6 @@
     chunk = hidden // replicas
     half = chunk // 2
     groups = Y_PAIR * NEAR
-    order = sorted(range(far), key=lambda i: (i % 2, i % (far // 2)))
     packed = (groups, TILES * far * half, LANES)
     with jax.named_scope("partials"):
         hint = pl.CostEstimate(flops=4 * 10**9, bytes_accessed=10**6, transcendentals=0)
@@ -202,34 +206,31 @@
         )(counts)
         (blocks,) = call(core_sum_kernel, [packed], [VMEM] * 3)(mask, keep, got)
     with jax.named_scope("near_sum"):
-        blocks = lax.all_to_all(blocks, ("pair", "near"), 0, 0, tiled=True)
-        (blocks,) = call(
-            functools.partial(near_sum_kernel, order), [(far, 1, TILES * half * LANES)], [VMEM]
-        )(blocks)
+        blocks = lax.all_to_all(blocks, ("near", "pair"), 0, 0, tiled=True)
+        (blocks,) = call(near_sum_kernel, [(far, 1, TILES * half * LANES)], [VMEM])(blocks)
     with jax.named_scope("far_sum"):
-        blocks = lax.all_to_all(
-            blocks, "far", 0, 0, axis_index_groups=[order], tiled=True
-        )
+        blocks = lax.all_to_all(blocks, "far", 0, 0, tiled=True)
+    with jax.named_scope("norm"):
+        total, squares = call(
+            functools.partial(square_kernel, sections * slots),
+            [(TILES, PAD_ROWS, LANES), (replicas, 1, LANES)],
+            [VMEM, VMEM],
+        )(mask, blocks)
+        squares = lax.all_to_all(squares, ("pair", "far", "near", "core"), 0, 0, tiled=True)
     with jax.named_scope("route"):
         (routed,) = call(
             functools.partial(route_kernel, slots),
             [(sections, PAD_ROWS, 2 * LANES)],
-            [VMEM, VMEM],
-            [pltpu.VMEM((TILES, PAD_ROWS, LANES), jnp.float32)],
-        )(mask, blocks)
+            [VMEM] * 3,
+        )(mask, total, squares)
         routed = lax.all_to_all(routed, "section", 0, 0, tiled=True)
-        owned, squares = call(
-            own_kernel, [(PAD_ROWS, 2 * LANES), (replicas, 1, LANES)], [VMEM]
-        )(routed)
-    with jax.named_scope("norm"):
-        squares = lax.all_to_all(squares, ("pair", "far", "near", "core"), 0, 0, tiled=True)
     with jax.named_scope("clip"):
         entries = sections * DEPTHS_PER_OWNER * hidden * rank
         (out,) = call(
             functools.partial(clip_kernel, entries),
             [(chunk, DEPTHS_PER_OWNER, rank)],
-            [VMEM, VMEM],
-        )(owned, squares)
+            [VMEM],
+        )(routed)
     return jnp.swapaxes(out, 0, 1)
 
 

time: 96.5 us -> 94.9 us (0.983)
  blocking collectives: 75 us -> 72.8 us
    all_to_all x1, blocking collectives: 26.1 us -> 21.4 us  [on_device(): lax.all_to_all(squares, ('pair', 'far', 'near', 'core'), 0, 0, tiled=True)]
    all_to_all x2, blocking collectives: 30.7 us -> 32.7 us  [the longest x1 20.4 us: on_device(): blocks = lax.all_to_all(blocks, 'far', 0, 0, tiled=True)]
where the time goes in v5:
time: 94.9 us; the launch traced here: 94 us
  blocking collectives  72.8 us (77%)
  starting transfers between devices  16 us (17%)
  Pallas kernels  2.91 us (3%)
  waiting for transfers between devices  1.12 us (1%)
  local copies, waits for them, and re-layouts  1.11 us (1%)
    all_to_all x1, blocking collectives, on_device(): lax.all_to_all(squares, ('pair', 'far', 'near', 'core'), 0, 0, tiled=True)  21.4 us
    all_to_all x1, blocking collectives, on_device(): blocks = lax.all_to_all(blocks, 'far', 0, 0, tiled=True)  20.4 us
    all_to_all x1, blocking collectives, on_device(): routed = lax.all_to_all(routed, 'section', 0, 0, tiled=True)  18.7 us
    ppermute x1, starting transfers between devices, on_device(): got = lax.ppermute(send, 'core', [(0, 1), (1, 0)])  16 us
    all_to_all x1, blocking collectives, on_device(): blocks = lax.all_to_all(blocks, ('near', 'pair'), 0, 0, tiled=True)  12.3 us
  transfers between devices with their start and end apart: 1, of which 1 were waited for; matrix products, arithmetic and copies ran while one was open for 0% of the time, Pallas kernels for 1%

profile of v5, /device:TPU:1, one launch (start us, length us, event | category | flops | bytes accessed | tf_op | source)
XLA Modules:
  0.0 94.0 jit_solution(9798886734041900403)
XLA Ops:
  0.0 0.0 copy-start.1
  0.0 0.0 copy-start
  0.0 0.0 copy-start.2
  0.0 0.8 copy-done.1
  0.8 0.2 partials.4.blocks_ref
  1.0 0.3 copy-done
  1.4 0.8 partials.5
  2.2 16.0 %collective-permute-start = (f32[4,336,128]{2,1,0:T(8,128)S(1)}, f32[4,336,128]{2,1,0:T(8,128)S(1)}, u32[]{:S(2)}, u32[]{:S(2)}) collective-permute-start(f32[4,336,128]{2,1,0:T(8,128)S(1)} %get-tuple-element.10), channel_id=1, source_target_pairs={{0,1},{1,0},{2,3},{3,2},{4,5},{5,4},{6,7},{7,6},{8,9},{9,8},{10,11... | collective-permute-start | bytes 2064392 | tf_op jit(solution)/shard_map/core_sum/ppermute | solution.py:203
  18.2 0.0 copy-done.2
  18.2 0.6 core_sum.2.mask_ref
  18.9 1.1 %collective-permute-done.got_ref = f32[4,336,128]{2,1,0:T(8,128)S(1)} collective-permute-done((f32[4,336,128]{2,1,0:T(8,128)S(1)}, f32[4,336,128]{2,1,0:T(8,128)S(1)}, u32[]{:S(2)}, u32[]{:S(2)}) %collective-permute-start) | collective-permute-done | bytes 688160 | tf_op jit(solution)/shard_map/core_sum/ppermute | solution.py:203
  20.0 0.1 core_sum.3
  20.1 12.3 %all_to_all.20.got_ref = f32[4,336,128]{2,1,0:T(8,128)S(1)} all-to-all(f32[4,336,128]{2,1,0:T(8,128)S(1)} %core_sum.3), channel_id=1, replica_groups=mesh['section'=16,'pair'=2,'far'=8,'near'=2,'core'=2] {'near','pair'}, dimensions={0} | all-to-all | bytes 1376256 | tf_op jit(solution)/shard_map/near_sum/all_to_all | solution.py:209
  32.3 0.1 near_sum.1
  32.5 20.4 %all_to_all.21.got_ref = f32[8,1,5376]{2,1,0:T(1,128)S(1)} all-to-all(f32[8,1,5376]{2,1,0:T(1,128)S(1)} %near_sum.1), channel_id=1, replica_groups=mesh['section'=16,'pair'=2,'far'=8,'near'=2,'core'=2] {'far'}, dimensions={0} | all-to-all | bytes 344064 | tf_op jit(solution)/shard_map/far_sum/all_to_all | solution.py:212
  52.9 0.1 norm.1
  53.0 21.4 %all_to_all.22.squares_ref = f32[64,1,128]{2,1,0:T(1,128)S(1)} all-to-all(f32[64,1,128]{2,1,0:T(1,128)S(1)} %get-tuple-element.12), channel_id=1, replica_groups=mesh['section'=16,'pair'=2,'far'=8,'near'=2,'core'=2] {'pair','far','nea..., dimensions={0} | all-to-all | bytes 65536 | tf_op jit(solution)/shard_map/norm/all_to_all | solution.py:219
  74.4 0.1 route.1
  74.5 18.7 %all_to_all.23.got_ref = f32[16,16,256]{2,1,0:T(8,128)S(1)} all-to-all(f32[16,16,256]{2,1,0:T(8,128)S(1)} %route.1), channel_id=1, replica_groups=mesh['section'=16,'pair'=2,'far'=8,'near'=2,'core'=2] {'section'}, dimensions={0} | all-to-all | bytes 524288 | tf_op jit(solution)/shard_map/route/all_to_all | solution.py:226
  93.2 0.8 clip.1
  (1 shorter events, 0.0 us)
Async XLA Ops:
  0.0 0.8 copy-start.1
  0.0 1.4 %copy-start = (bf16[1,3,128,1792]{3,2,1,0:T(8,128)(2,1)S(1)}, bf16[1,3,128,1792]{3,2,1,0:T(8,128)(2,1)}, u32[]{:S(2)}) copy-start(bf16[1,3,128,1792]{3,2,1,0:T(8,128)(2,1)} %param.4) | copy-start | bytes 4128772
  0.0 18.2 %copy-start.2 = (s32[16]{0:T(128)S(1)}, s32[16]{0:T(128)}, u32[]{:S(2)}) copy-start(s32[16]{0:T(128)} %counts.1) | copy-start | bytes 196
  2.2 17.8 %collective-permute-start = (f32[4,336,128]{2,1,0:T(8,128)S(1)}, f32[4,336,128]{2,1,0:T(8,128)S(1)}, u32[]{:S(2)}, u32[]{:S(2)}) collective-permute-start(f32[4,336,128]{2,1,0:T(8,128)S(1)} %get-tuple-element.10), channel_id=1, source_target_pairs={{0,1},{1,0},{2,3},{3,2},{4,5},{5,4},{6,7},{7,6},{8,9},{9,8},{10,11... | collective-permute-start | bytes 2064392 | tf_op jit(solution)/shard_map/core_sum/ppermute | solution.py:203

commit v6 on v5

--- a/solution.py
+++ b/solution.py
@@ -89,14 +89,14 @@
     out_ref[...] = keep_ref[...] + got_ref[...]
 
 
-def near_sum_kernel(got_ref, out_ref):
+def near_sum_kernel(order, got_ref, out_ref):
     total = jnp.sum(got_ref[...], axis=0)
     far = out_ref.shape[0]
     half = total.shape[0] // (TILES * far)
     for i in range(far):
         for t in range(TILES):
             for r in range(half):
-                row = (t * far + i) * half + r
+                row = (t * far + order[i]) * half + r
                 out_ref[i, :, pl.ds((t * half + r) * LANES, LANES)] = total[row : row + 1, :]
 
 
@@ -183,6 +183,7 @@
     chunk = hidden // replicas
     half = chunk // 2
     groups = Y_PAIR * NEAR
+    order = sorted(range(far), key=lambda i: (i * (far // 2 - 1)) % far)
     packed = (groups, TILES * far * half, LANES)
     with jax.named_scope("partials"):
         hint = pl.CostEstimate(flops=4 * 10**9, bytes_accessed=10**6, transcendentals=0)
@@ -207,9 +208,13 @@
         (blocks,) = call(core_sum_kernel, [packed], [VMEM] * 3)(mask, keep, got)
     with jax.named_scope("near_sum"):
         blocks = lax.all_to_all(blocks, ("near", "pair"), 0, 0, tiled=True)
-        (blocks,) = call(near_sum_kernel, [(far, 1, TILES * half * LANES)], [VMEM])(blocks)
+        (blocks,) = call(
+            functools.partial(near_sum_kernel, order), [(far, 1, TILES * half * LANES)], [VMEM]
+        )(blocks)
     with jax.named_scope("far_sum"):
-        blocks = lax.all_to_all(blocks, "far", 0, 0, tiled=True)
+        blocks = lax.all_to_all(
+            blocks, "far", 0, 0, axis_index_groups=[order], tiled=True
+        )
     with jax.named_scope("norm"):
         total, squares = call(
             functools.partial(square_kernel, sections * slots),

time: 94.9 us -> 94.6 us (level)
  no operation moved by 1% of the time
where the time goes in v6:
time: 94.6 us; the launch traced here: 93.8 us
  blocking collectives  72.5 us (77%)
  starting transfers between devices  16 us (17%)
  Pallas kernels  2.91 us (3%)
  waiting for transfers between devices  1.12 us (1%)
  local copies, waits for them, and re-layouts  1.11 us (1%)
    all_to_all x1, blocking collectives, on_device(): lax.all_to_all(blocks, 'far', 0, 0, axis_index_groups=[order], tiled=True)  20.8 us
    all_to_all x1, blocking collectives, on_device(): lax.all_to_all(squares, ('pair', 'far', 'near', 'core'), 0, 0, tiled=True)  20.8 us
    all_to_all x1, blocking collectives, on_device(): routed = lax.all_to_all(routed, 'section', 0, 0, tiled=True)  18.7 us
    ppermute x1, starting transfers between devices, on_device(): got = lax.ppermute(send, 'core', [(0, 1), (1, 0)])  16 us
    all_to_all x1, blocking collectives, on_device(): blocks = lax.all_to_all(blocks, ('near', 'pair'), 0, 0, tiled=True)  12.3 us
  transfers between devices with their start and end apart: 1, of which 1 were waited for; matrix products, arithmetic and copies ran while one was open for 0% of the time, Pallas kernels for 1%

profile of v6, /device:TPU:1, one launch (start us, length us, event | category | flops | bytes accessed | tf_op | source)
XLA Modules:
  0.0 93.8 jit_solution(2341929095580400690)
XLA Ops:
  0.0 0.0 copy-start.1
  0.0 0.0 copy-start
  0.0 0.0 copy-start.2
  0.0 0.8 copy-done.1
  0.8 0.2 partials.4.blocks_ref
  1.0 0.3 copy-done
  1.4 0.8 partials.5
  2.2 16.0 %collective-permute-start = (f32[4,336,128]{2,1,0:T(8,128)S(1)}, f32[4,336,128]{2,1,0:T(8,128)S(1)}, u32[]{:S(2)}, u32[]{:S(2)}) collective-permute-start(f32[4,336,128]{2,1,0:T(8,128)S(1)} %get-tuple-element.10), channel_id=1, source_target_pairs={{0,1},{1,0},{2,3},{3,2},{4,5},{5,4},{6,7},{7,6},{8,9},{9,8},{10,11... | collective-permute-start | bytes 2064392 | tf_op jit(solution)/shard_map/core_sum/ppermute | solution.py:204
  18.2 0.0 copy-done.2
  18.2 0.6 core_sum.2.mask_ref
  18.9 1.1 %collective-permute-done.got_ref = f32[4,336,128]{2,1,0:T(8,128)S(1)} collective-permute-done((f32[4,336,128]{2,1,0:T(8,128)S(1)}, f32[4,336,128]{2,1,0:T(8,128)S(1)}, u32[]{:S(2)}, u32[]{:S(2)}) %collective-permute-start) | collective-permute-done | bytes 688160 | tf_op jit(solution)/shard_map/core_sum/ppermute | solution.py:204
  20.0 0.1 core_sum.3
  20.1 12.3 %all_to_all.20.got_ref = f32[4,336,128]{2,1,0:T(8,128)S(1)} all-to-all(f32[4,336,128]{2,1,0:T(8,128)S(1)} %core_sum.3), channel_id=1, replica_groups=mesh['section'=16,'pair'=2,'far'=8,'near'=2,'core'=2] {'near','pair'}, dimensions={0} | all-to-all | bytes 1376256 | tf_op jit(solution)/shard_map/near_sum/all_to_all | solution.py:210
  32.3 0.1 near_sum.1
  32.5 20.8 %all_to_all.21.got_ref = f32[8,1,5376]{2,1,0:T(1,128)S(1)} all-to-all(f32[8,1,5376]{2,1,0:T(1,128)S(1)} %near_sum.1), channel_id=1, replica_groups={{0,12,24,4,16,28,8,20},{1,13,25,5,17,29,9,21},{2,14,26,6,18,30,10,22},{..., dimensions={0} | all-to-all | bytes 344064 | tf_op jit(solution)/shard_map/far_sum/all_to_all | solution.py:215
  53.2 0.1 norm.1
  53.4 20.8 %all_to_all.22.squares_ref = f32[64,1,128]{2,1,0:T(1,128)S(1)} all-to-all(f32[64,1,128]{2,1,0:T(1,128)S(1)} %get-tuple-element.12), channel_id=1, replica_groups=mesh['section'=16,'pair'=2,'far'=8,'near'=2,'core'=2] {'pair','far','nea..., dimensions={0} | all-to-all | bytes 65536 | tf_op jit(solution)/shard_map/norm/all_to_all | solution.py:224
  74.1 0.1 route.1
  74.3 18.7 %all_to_all.23.got_ref = f32[16,16,256]{2,1,0:T(8,128)S(1)} all-to-all(f32[16,16,256]{2,1,0:T(8,128)S(1)} %route.1), channel_id=1, replica_groups=mesh['section'=16,'pair'=2,'far'=8,'near'=2,'core'=2] {'section'}, dimensions={0} | all-to-all | bytes 524288 | tf_op jit(solution)/shard_map/route/all_to_all | solution.py:231
  93.0 0.8 clip.1
  (1 shorter events, 0.0 us)
Async XLA Ops:
  0.0 0.8 copy-start.1
  0.0 1.4 %copy-start = (bf16[1,3,128,1792]{3,2,1,0:T(8,128)(2,1)S(1)}, bf16[1,3,128,1792]{3,2,1,0:T(8,128)(2,1)}, u32[]{:S(2)}) copy-start(bf16[1,3,128,1792]{3,2,1,0:T(8,128)(2,1)} %param.4) | copy-start | bytes 4128772
  0.0 18.2 %copy-start.2 = (s32[16]{0:T(128)S(1)}, s32[16]{0:T(128)}, u32[]{:S(2)}) copy-start(s32[16]{0:T(128)} %counts.1) | copy-start | bytes 196
  2.2 17.8 %collective-permute-start = (f32[4,336,128]{2,1,0:T(8,128)S(1)}, f32[4,336,128]{2,1,0:T(8,128)S(1)}, u32[]{:S(2)}, u32[]{:S(2)}) collective-permute-start(f32[4,336,128]{2,1,0:T(8,128)S(1)} %get-tuple-element.10), channel_id=1, source_target_pairs={{0,1},{1,0},{2,3},{3,2},{4,5},{5,4},{6,7},{7,6},{8,9},{9,8},{10,11... | collective-permute-start | bytes 2064392 | tf_op jit(solution)/shard_map/core_sum/ppermute | solution.py:204

commit v7 on v6

--- a/solution.py
+++ b/solution.py
@@ -140,7 +140,9 @@
 
 
 def route_kernel(slots, mask_ref, total_ref, squares_ref, out_ref):
-    owners, rows, _ = out_ref.shape
+    owners, _, size = out_ref.shape
+    _, rows, _ = total_ref.shape
+    half = (size // LANES - 1) // 2
     base = owners * slots
     first, last = mask_ref[pl.ds(base, 1), :], mask_ref[pl.ds(base + 1, 1), :]
     live = (first, last, first)
@@ -151,25 +153,30 @@
     both = [jnp.where(left, x, y) for x, y in zip(tiles, turned)]
     flip = [jnp.where(left, y, x) for x, y in zip(tiles, turned)]
     halves = ((both[0], flip[0], both[1]), (both[2], flip[2], flip[1]))
-    bottom = lax.broadcasted_iota(jnp.int32, (rows, LANES), 0) == rows - 1
-    blank = jnp.where(bottom, squares, 0.0)
     for e in range(owners):
         for h in range(2):
-            value = blank
+            value = jnp.zeros((rows, LANES), jnp.float32)
             for k in range(slots):
                 value = value + mask_ref[pl.ds(e * slots + k, 1), :] * halves[h][k]
-            out_ref[e, :, pl.ds(h * LANES, LANES)] = value
-
-
-def clip_kernel(entries, got_ref, out_ref):
+            for r in range(half):
+                out_ref[e, :, pl.ds((h * half + r) * LANES, LANES)] = value[r : r + 1, :]
+        out_ref[e, :, pl.ds(2 * half * LANES, LANES)] = squares
+
+
+def clip_kernel(entries, got_ref, out_ref, owned_ref):
     chunk, _, rank = out_ref.shape
     half = chunk // 2
-    owned = jnp.sum(got_ref[...], axis=0)
-    square = jnp.sum(owned[owned.shape[0] - 1 :, :LANES], axis=1, keepdims=True)
+    flat = jnp.sum(got_ref[...], axis=0)
+    owned_ref[...] = jnp.zeros_like(owned_ref)
+    for h in range(2):
+        for r in range(half):
+            at = (h * half + r) * LANES
+            owned_ref[h, pl.ds(r, 1), :] = flat[:, at : at + LANES]
+    square = jnp.sum(flat[:, chunk * LANES :], axis=1, keepdims=True)
     factor = jnp.minimum(1.0, 0.5 / jnp.sqrt(square / entries + 1e-06))
-    owned = owned * jnp.broadcast_to(factor, owned.shape)
+    factor = jnp.broadcast_to(factor, owned_ref.shape[1:])
     for h in range(2):
-        tile = owned[:, h * LANES : (h + 1) * LANES]
+        tile = owned_ref[h] * factor
         turned = pltpu.roll(tile, rank, 1)
         out_ref[pl.ds(half * h, half), 0, :] = tile[:half, :rank]
         out_ref[pl.ds(half * h, half), 1, :] = turned[:half, :rank]
@@ -225,7 +232,7 @@
     with jax.named_scope("route"):
         (routed,) = call(
             functools.partial(route_kernel, slots),
-            [(sections, PAD_ROWS, 2 * LANES)],
+            [(sections, 1, (chunk + 1) * LANES)],
             [VMEM] * 3,
         )(mask, total, squares)
         routed = lax.all_to_all(routed, "section", 0, 0, tiled=True)
@@ -235,6 +242,7 @@
             functools.partial(clip_kernel, entries),
             [(chunk, DEPTHS_PER_OWNER, rank)],
             [VMEM],
+            [pltpu.VMEM((2, PAD_ROWS, LANES), jnp.float32)],
         )(routed)
     return jnp.swapaxes(out, 0, 1)
 

time: 94.6 us -> 94.3 us (level)
  no operation moved by 1% of the time
where the time goes in v7:
time: 94.3 us; the launch traced here: 93.5 us
  blocking collectives  72 us (76%)
  starting transfers between devices  16 us (17%)
  Pallas kernels  3.09 us (3%)
  waiting for transfers between devices  1.12 us (1%)
  local copies, waits for them, and re-layouts  1.11 us (1%)
    all_to_all x1, blocking collectives, on_device(): lax.all_to_all(blocks, 'far', 0, 0, axis_index_groups=[order], tiled=True)  20.8 us
    all_to_all x1, blocking collectives, on_device(): lax.all_to_all(squares, ('pair', 'far', 'near', 'core'), 0, 0, tiled=True)  20.8 us
    all_to_all x1, blocking collectives, on_device(): routed = lax.all_to_all(routed, 'section', 0, 0, tiled=True)  18.2 us
    ppermute x1, starting transfers between devices, on_device(): got = lax.ppermute(send, 'core', [(0, 1), (1, 0)])  16 us
    all_to_all x1, blocking collectives, on_device(): blocks = lax.all_to_all(blocks, ('near', 'pair'), 0, 0, tiled=True)  12.3 us
  transfers between devices with their start and end apart: 1, of which 1 were waited for; matrix products, arithmetic and copies ran while one was open for 0% of the time, Pallas kernels for 1%

profile of v7, /device:TPU:1, one launch (start us, length us, event | category | flops | bytes accessed | tf_op | source)
XLA Modules:
  0.0 93.5 jit_solution(8366189204501261947)
XLA Ops:
  0.0 0.0 copy-start.1
  0.0 0.0 copy-start
  0.0 0.0 copy-start.2
  0.0 0.8 copy-done.1
  0.8 0.2 partials.4.blocks_ref
  1.0 0.3 copy-done
  1.4 0.8 partials.5
  2.2 16.0 %collective-permute-start = (f32[4,336,128]{2,1,0:T(8,128)S(1)}, f32[4,336,128]{2,1,0:T(8,128)S(1)}, u32[]{:S(2)}, u32[]{:S(2)}) collective-permute-start(f32[4,336,128]{2,1,0:T(8,128)S(1)} %get-tuple-element.10), channel_id=1, source_target_pairs={{0,1},{1,0},{2,3},{3,2},{4,5},{5,4},{6,7},{7,6},{8,9},{9,8},{10,11... | collective-permute-start | bytes 2064392 | tf_op jit(solution)/shard_map/core_sum/ppermute | solution.py:211
  18.2 0.0 copy-done.2
  18.2 0.6 core_sum.2.mask_ref
  18.9 1.1 %collective-permute-done.got_ref = f32[4,336,128]{2,1,0:T(8,128)S(1)} collective-permute-done((f32[4,336,128]{2,1,0:T(8,128)S(1)}, f32[4,336,128]{2,1,0:T(8,128)S(1)}, u32[]{:S(2)}, u32[]{:S(2)}) %collective-permute-start) | collective-permute-done | bytes 688160 | tf_op jit(solution)/shard_map/core_sum/ppermute | solution.py:211
  20.0 0.1 core_sum.3
  20.1 12.3 %all_to_all.20.got_ref = f32[4,336,128]{2,1,0:T(8,128)S(1)} all-to-all(f32[4,336,128]{2,1,0:T(8,128)S(1)} %core_sum.3), channel_id=1, replica_groups=mesh['section'=16,'pair'=2,'far'=8,'near'=2,'core'=2] {'near','pair'}, dimensions={0} | all-to-all | bytes 1376256 | tf_op jit(solution)/shard_map/near_sum/all_to_all | solution.py:217
  32.3 0.1 near_sum.1
  32.5 20.8 %all_to_all.21.got_ref = f32[8,1,5376]{2,1,0:T(1,128)S(1)} all-to-all(f32[8,1,5376]{2,1,0:T(1,128)S(1)} %near_sum.1), channel_id=1, replica_groups={{0,12,24,4,16,28,8,20},{1,13,25,5,17,29,9,21},{2,14,26,6,18,30,10,22},{..., dimensions={0} | all-to-all | bytes 344064 | tf_op jit(solution)/shard_map/far_sum/all_to_all | solution.py:222
  53.2 0.1 norm.1
  53.4 20.8 %all_to_all.22.squares_ref = f32[64,1,128]{2,1,0:T(1,128)S(1)} all-to-all(f32[64,1,128]{2,1,0:T(1,128)S(1)} %get-tuple-element.12), channel_id=1, replica_groups=mesh['section'=16,'pair'=2,'far'=8,'near'=2,'core'=2] {'pair','far','nea..., dimensions={0} | all-to-all | bytes 65536 | tf_op jit(solution)/shard_map/norm/all_to_all | solution.py:231
  74.1 0.2 route.1
  74.4 18.2 %all_to_all.23.got_ref = f32[16,1,3712]{2,1,0:T(1,128)S(1)} all-to-all(f32[16,1,3712]{2,1,0:T(1,128)S(1)} %route.1), channel_id=1, replica_groups=mesh['section'=16,'pair'=2,'far'=8,'near'=2,'core'=2] {'section'}, dimensions={0} | all-to-all | bytes 475136 | tf_op jit(solution)/shard_map/route/all_to_all | solution.py:238
  92.6 0.9 clip.1
  (1 shorter events, 0.0 us)
Async XLA Ops:
  0.0 0.8 copy-start.1
  0.0 1.4 %copy-start = (bf16[1,3,128,1792]{3,2,1,0:T(8,128)(2,1)S(1)}, bf16[1,3,128,1792]{3,2,1,0:T(8,128)(2,1)}, u32[]{:S(2)}) copy-start(bf16[1,3,128,1792]{3,2,1,0:T(8,128)(2,1)} %param.4) | copy-start | bytes 4128772
  0.0 18.2 %copy-start.2 = (s32[16]{0:T(128)S(1)}, s32[16]{0:T(128)}, u32[]{:S(2)}) copy-start(s32[16]{0:T(128)} %counts.1) | copy-start | bytes 196
  2.2 17.8 %collective-permute-start = (f32[4,336,128]{2,1,0:T(8,128)S(1)}, f32[4,336,128]{2,1,0:T(8,128)S(1)}, u32[]{:S(2)}, u32[]{:S(2)}) collective-permute-start(f32[4,336,128]{2,1,0:T(8,128)S(1)} %get-tuple-element.10), channel_id=1, source_target_pairs={{0,1},{1,0},{2,3},{3,2},{4,5},{5,4},{6,7},{7,6},{8,9},{9,8},{10,11... | collective-permute-start | bytes 2064392 | tf_op jit(solution)/shard_map/core_sum/ppermute | solution.py:211

commit v8 on v7

--- a/solution.py
+++ b/solution.py
@@ -190,7 +190,7 @@
     chunk = hidden // replicas
     half = chunk // 2
     groups = Y_PAIR * NEAR
-    order = sorted(range(far), key=lambda i: (i * (far // 2 - 1)) % far)
+    order = sorted(range(far), key=lambda i: (i * (far // 2 + 1)) % far)
     packed = (groups, TILES * far * half, LANES)
     with jax.named_scope("partials"):
         hint = pl.CostEstimate(flops=4 * 10**9, bytes_accessed=10**6, transcendentals=0)

time: 94.3 us -> 94.6 us (level)
  no operation moved by 1% of the time
where the time goes in v8:
time: 94.6 us; the launch traced here: 93.7 us
  blocking collectives  72.3 us (76%)
  starting transfers between devices  16 us (17%)
  Pallas kernels  3.09 us (3%)
  waiting for transfers between devices  1.12 us (1%)
  local copies, waits for them, and re-layouts  1.11 us (1%)
    all_to_all x1, blocking collectives, on_device(): lax.all_to_all(squares, ('pair', 'far', 'near', 'core'), 0, 0, tiled=True)  21.4 us
    all_to_all x1, blocking collectives, on_device(): lax.all_to_all(blocks, 'far', 0, 0, axis_index_groups=[order], tiled=True)  20.4 us
    all_to_all x1, blocking collectives, on_device(): routed = lax.all_to_all(routed, 'section', 0, 0, tiled=True)  18.2 us
    ppermute x1, starting transfers between devices, on_device(): got = lax.ppermute(send, 'core', [(0, 1), (1, 0)])  16 us
    all_to_all x1, blocking collectives, on_device(): blocks = lax.all_to_all(blocks, ('near', 'pair'), 0, 0, tiled=True)  12.3 us
  transfers between devices with their start and end apart: 1, of which 1 were waited for; matrix products, arithmetic and copies ran while one was open for 0% of the time, Pallas kernels for 1%

profile of v8, /device:TPU:1, one launch (start us, length us, event | category | flops | bytes accessed | tf_op | source)
XLA Modules:
  0.0 93.7 jit_solution(12964183609407042779)
XLA Ops:
  0.0 0.0 copy-start.1
  0.0 0.0 copy-start
  0.0 0.0 copy-start.2
  0.0 0.8 copy-done.1
  0.8 0.2 partials.4.blocks_ref
  1.0 0.3 copy-done
  1.4 0.8 partials.5
  2.2 16.0 %collective-permute-start = (f32[4,336,128]{2,1,0:T(8,128)S(1)}, f32[4,336,128]{2,1,0:T(8,128)S(1)}, u32[]{:S(2)}, u32[]{:S(2)}) collective-permute-start(f32[4,336,128]{2,1,0:T(8,128)S(1)} %get-tuple-element.10), channel_id=1, source_target_pairs={{0,1},{1,0},{2,3},{3,2},{4,5},{5,4},{6,7},{7,6},{8,9},{9,8},{10,11... | collective-permute-start | bytes 2064392 | tf_op jit(solution)/shard_map/core_sum/ppermute | solution.py:211
  18.2 0.0 copy-done.2
  18.2 0.6 core_sum.2.mask_ref
  18.9 1.1 %collective-permute-done.got_ref = f32[4,336,128]{2,1,0:T(8,128)S(1)} collective-permute-done((f32[4,336,128]{2,1,0:T(8,128)S(1)}, f32[4,336,128]{2,1,0:T(8,128)S(1)}, u32[]{:S(2)}, u32[]{:S(2)}) %collective-permute-start) | collective-permute-done | bytes 688160 | tf_op jit(solution)/shard_map/core_sum/ppermute | solution.py:211
  20.0 0.1 core_sum.3
  20.1 12.3 %all_to_all.20.got_ref = f32[4,336,128]{2,1,0:T(8,128)S(1)} all-to-all(f32[4,336,128]{2,1,0:T(8,128)S(1)} %core_sum.3), channel_id=1, replica_groups=mesh['section'=16,'pair'=2,'far'=8,'near'=2,'core'=2] {'near','pair'}, dimensions={0} | all-to-all | bytes 1376256 | tf_op jit(solution)/shard_map/near_sum/all_to_all | solution.py:217
  32.3 0.1 near_sum.1
  32.5 20.4 %all_to_all.21.got_ref = f32[8,1,5376]{2,1,0:T(1,128)S(1)} all-to-all(f32[8,1,5376]{2,1,0:T(1,128)S(1)} %near_sum.1), channel_id=1, replica_groups={{0,20,8,28,16,4,24,12},{1,21,9,29,17,5,25,13},{2,22,10,30,18,6,26,14},{..., dimensions={0} | all-to-all | bytes 344064 | tf_op jit(solution)/shard_map/far_sum/all_to_all | solution.py:222
  52.9 0.1 norm.1
  53.0 21.4 %all_to_all.22.squares_ref = f32[64,1,128]{2,1,0:T(1,128)S(1)} all-to-all(f32[64,1,128]{2,1,0:T(1,128)S(1)} %get-tuple-element.12), channel_id=1, replica_groups=mesh['section'=16,'pair'=2,'far'=8,'near'=2,'core'=2] {'pair','far','nea..., dimensions={0} | all-to-all | bytes 65536 | tf_op jit(solution)/shard_map/norm/all_to_all | solution.py:231
  74.4 0.2 route.1
  74.7 18.2 %all_to_all.23.got_ref = f32[16,1,3712]{2,1,0:T(1,128)S(1)} all-to-all(f32[16,1,3712]{2,1,0:T(1,128)S(1)} %route.1), channel_id=1, replica_groups=mesh['section'=16,'pair'=2,'far'=8,'near'=2,'core'=2] {'section'}, dimensions={0} | all-to-all | bytes 475136 | tf_op jit(solution)/shard_map/route/all_to_all | solution.py:238
  92.9 0.9 clip.1
  (1 shorter events, 0.0 us)
Async XLA Ops:
  0.0 0.8 copy-start.1
  0.0 1.4 %copy-start = (bf16[1,3,128,1792]{3,2,1,0:T(8,128)(2,1)S(1)}, bf16[1,3,128,1792]{3,2,1,0:T(8,128)(2,1)}, u32[]{:S(2)}) copy-start(bf16[1,3,128,1792]{3,2,1,0:T(8,128)(2,1)} %param.4) | copy-start | bytes 4128772
  0.0 18.2 %copy-start.2 = (s32[16]{0:T(128)S(1)}, s32[16]{0:T(128)}, u32[]{:S(2)}) copy-start(s32[16]{0:T(128)} %counts.1) | copy-start | bytes 196
  2.2 17.8 %collective-permute-start = (f32[4,336,128]{2,1,0:T(8,128)S(1)}, f32[4,336,128]{2,1,0:T(8,128)S(1)}, u32[]{:S(2)}, u32[]{:S(2)}) collective-permute-start(f32[4,336,128]{2,1,0:T(8,128)S(1)} %get-tuple-element.10), channel_id=1, source_target_pairs={{0,1},{1,0},{2,3},{3,2},{4,5},{5,4},{6,7},{7,6},{8,9},{9,8},{10,11... | collective-permute-start | bytes 2064392 | tf_op jit(solution)/shard_map/core_sum/ppermute | solution.py:211
